TPU v7x, 256 devices: a whole 4x4x8 slice. The times are simulated.
256 devices in a mesh: prompt: 8 (over z_lo, core), resp: 32 (over x, y, z_hi).
Axes of the slice: x: 4, y: 4, z: 8 (z_hi: 2, z_lo: 4; z = z_hi * 4 + z_lo), core: 2. Of those that a mesh axis runs over, the one named last changes fastest.
Arguments:
- prompt_hidden: bfloat16 [16, 3072, 5120], P('prompt', 'resp'), may hold values from -6 to 6
- prompt_keys: bfloat16 [16, 3072, 128], P('prompt', 'resp'), may hold values from -6 to 6
- prompt_values: bfloat16 [16, 3072, 128], P('prompt', 'resp'), may hold values from -6 to 6
- resp_hidden: bfloat16 [8, 2048, 5120], P('prompt', 'resp'), may hold values from -6 to 6
- resp_queries: bfloat16 [8, 2048, 1024], P('prompt', 'resp'), may hold values from -180 to 180
- resp_keys: bfloat16 [8, 2048, 128], P('prompt', 'resp'), may hold values from -6 to 6
- resp_values: bfloat16 [8, 2048, 128], P('prompt', 'resp'), may hold values from -6 to 6
- cotangent: bfloat16 [8, 2048, 1024], P('prompt', 'resp'), may hold values from -6 to 6
- rewards: float32 [8, 32], P('prompt', 'resp'), may hold values from -4 to 4
- resp_prompt: int32 [8, 32], P('prompt', 'resp'), may hold values from 0 to 1, as said below
- resp_len: int32 [8, 32], P('prompt', 'resp'), may hold values from 1 to 64, as said below
- prompt_tenant: int32 [16], P('prompt'), may hold values from 0 to 7
- q_down: bfloat16 [8, 5120, 16], replicated, may hold values from -0.078125 to 0.078125
- q_up: bfloat16 [8, 16, 1024], replicated, may hold values from -1.5 to 1.5
- v_down: bfloat16 [8, 5120, 16], replicated, may hold values from -0.078125 to 0.078125
- v_up: bfloat16 [8, 16, 128], replicated, may hold values from -1.5 to 1.5
Outputs:
- attn_out: bfloat16 [8, 2048, 1024], P('prompt', 'resp')
- grad_q_down: float32 [8, 5120, 16], replicated
- grad_q_up: float32 [8, 16, 1024], replicated
- grad_v_down: float32 [8, 5120, 16], replicated
- grad_v_up: float32 [8, 16, 128], replicated
Inputs may be any that keep to these rules, and one draw needn't show every extreme that they name: `resp_len`: in every group one response has exactly 64 tokens; slots at or beyond a response's length are padding. `resp_prompt`: in one group every response continues prompt 1; in every other group some response continues prompt 0.
All inputs are finite; a program needn't handle non-finite values.
Results may differ from a plain program's by a relative error of at most 0.023.
Values may be sent and summed in bfloat16 or wider, within the bound.
A program may use at most 256 MiB of HBM per device.

v0:
```python
import jax
import jax.numpy as jnp
from jax import lax
from jax.sharding import PartitionSpec as P

adapter_scale = 2.0
contract_rows = (((0,), (0,)), ((), ()))


def lift_values(hidden_rows, frozen_output, down, up_projection):
    low_rank_rows = jnp.dot(hidden_rows, down, preferred_element_type=jnp.float32).astype(
        jnp.bfloat16
    )
    adapter_output = frozen_output.astype(jnp.float32) + adapter_scale * jnp.dot(
        low_rank_rows, up_projection, preferred_element_type=jnp.float32
    )
    return (low_rank_rows, adapter_output.astype(jnp.bfloat16))


def prompt_terms(hidden_rows, low_rank_rows, values_gradient, up_projection):
    hidden_prompt = lax.Precision.HIGHEST
    up_gradient = adapter_scale * jnp.dot(
        low_rank_rows.astype(jnp.float32).T, values_gradient, precision=hidden_prompt
    )
    backward_result = jnp.dot(
        values_gradient, up_projection.astype(jnp.float32).T, precision=hidden_prompt
    ).astype(jnp.bfloat16)
    down_gradient = adapter_scale * jnp.dot(
        hidden_rows.T, backward_result, preferred_element_type=jnp.float32
    )
    return (down_gradient, up_gradient)


def per_device(
    prompt_hidden,
    prompt_keys,
    prompt_values,
    resp_hidden,
    resp_queries,
    resp_keys,
    resp_values,
    cotangent,
    rewards,
    resp_prompt,
    resp_len,
    prompt_tenant,
    q_down,
    q_up,
    v_down,
    v_up,
):
    local_prompts = prompt_hidden.shape[0]
    head_dim = prompt_keys.shape[2]
    tenant_count = q_down.shape[0]
    rank = q_down.shape[2]
    response_input = resp_hidden[0]
    slots = response_input.shape[0]
    heads = resp_queries.shape[2] // head_dim
    factor = head_dim ** (-0.5)
    hidden_prompt = lax.Precision.HIGHEST
    lowered_all = []
    lifted_all = []
    for slot in range(local_prompts):
        owner = prompt_tenant[slot]
        low_rank_rows, lifted = lift_values(
            prompt_hidden[slot], prompt_values[slot], v_down[owner], v_up[owner]
        )
        lowered_all.append(low_rank_rows)
        lifted_all.append(lifted)
    lifted_stack = jnp.stack(lifted_all)
    keys_all, values_all = (
        lax.all_gather(prompt_keys, "resp", axis=1, tiled=True),
        lax.all_gather(lifted_stack, "resp", axis=1, tiled=True),
    )
    chosen = resp_prompt[0, 0]
    length = resp_len[0, 0]
    reward = rewards[0, 0]
    picked = (jnp.arange(local_prompts) == chosen).astype(jnp.float32)
    sums, counts = lax.psum((picked * reward, picked), "resp")
    means = sums / jnp.maximum(counts, 1.0)
    weight = -(reward - jnp.sum(picked * means)) / slots
    tenant = prompt_tenant[chosen]
    a_query = q_down[tenant]
    query_up_matrix = q_up[tenant]
    a_value = v_down[tenant]
    b_value = v_up[tenant]
    keys_p = keys_all[chosen]
    values_p = values_all[chosen]
    query_low_rank = jnp.dot(response_input, a_query, preferred_element_type=jnp.float32).astype(
        jnp.bfloat16
    )
    query_rows = (
        resp_queries[0].astype(jnp.float32)
        + adapter_scale
        * jnp.dot(query_low_rank, query_up_matrix, preferred_element_type=jnp.float32)
    ).astype(jnp.bfloat16)
    value_low_rank, own_values = lift_values(response_input, resp_values[0], a_value, b_value)
    base_key = resp_keys[0]
    q_rows = query_rows.reshape(slots * heads, head_dim)
    score_p = jnp.dot(q_rows, keys_p.T, preferred_element_type=jnp.float32) * factor
    score_s = jnp.dot(q_rows, base_key.T, preferred_element_type=jnp.float32) * factor
    q_pos = jnp.arange(slots * heads) // heads
    k_pos = jnp.arange(slots)
    allowed = (k_pos[None, :] <= q_pos[:, None]) & (k_pos[None, :] < length)
    highest = jnp.maximum(
        jnp.max(score_p, axis=1), jnp.max(jnp.where(allowed, score_s, -1e30), axis=1)
    )[:, None]
    exp_p = jnp.exp(score_p - highest)
    exp_s = jnp.where(allowed, jnp.exp(score_s - highest), 0.0)
    totals = (jnp.sum(exp_p, axis=1) + jnp.sum(exp_s, axis=1))[:, None]
    prob_p = exp_p / totals
    prob_s = exp_s / totals
    weight_p = prob_p.astype(jnp.bfloat16)
    weight_s = prob_s.astype(jnp.bfloat16)
    attended = jnp.dot(weight_p, values_p, preferred_element_type=jnp.float32) + jnp.dot(
        weight_s, own_values, preferred_element_type=jnp.float32
    )
    attn_out = attended.astype(jnp.bfloat16).reshape(1, slots, heads * head_dim)
    live = (jnp.arange(slots) < length).astype(jnp.float32)
    upstream = (
        (cotangent[0].astype(jnp.float32) * (weight * live)[:, None])
        .astype(jnp.bfloat16)
        .reshape(slots * heads, head_dim)
    )
    delta = jnp.sum(upstream.astype(jnp.float32) * attended, axis=1, keepdims=True)
    grad_sp = (
        prob_p * (jnp.dot(upstream, values_p.T, preferred_element_type=jnp.float32) - delta)
    ).astype(jnp.bfloat16)
    grad_ss = (
        prob_s * (jnp.dot(upstream, own_values.T, preferred_element_type=jnp.float32) - delta)
    ).astype(jnp.bfloat16)
    query_gradient = (
        (
            (
                jnp.dot(grad_sp, keys_p, preferred_element_type=jnp.float32)
                + jnp.dot(grad_ss, base_key, preferred_element_type=jnp.float32)
            )
            * factor
        )
        .astype(jnp.bfloat16)
        .reshape(slots, heads * head_dim)
    )
    attention_output_gradient = lax.dot_general(
        weight_s, upstream, contract_rows, preferred_element_type=jnp.float32
    ).astype(jnp.bfloat16)
    query_up_gradient = adapter_scale * jnp.dot(
        query_low_rank.T, query_gradient, preferred_element_type=jnp.float32
    )
    query_backward = jnp.dot(
        query_gradient, query_up_matrix.T, preferred_element_type=jnp.float32
    ).astype(jnp.bfloat16)
    query_down_gradient = adapter_scale * jnp.dot(
        response_input.T, query_backward, preferred_element_type=jnp.float32
    )
    value_up_gradient = adapter_scale * jnp.dot(
        value_low_rank.T, attention_output_gradient, preferred_element_type=jnp.float32
    )
    value_backward = jnp.dot(
        attention_output_gradient, b_value.T, preferred_element_type=jnp.float32
    ).astype(jnp.bfloat16)
    value_down_gradient = adapter_scale * jnp.dot(
        response_input.T, value_backward, preferred_element_type=jnp.float32
    )
    down_terms = []
    up_terms = []

    def prompt_term():
        part_grad = lax.dot_general(
            weight_p, upstream, contract_rows, preferred_element_type=jnp.float32
        )
        return jnp.concatenate([picked[slot] * part_grad for slot in range(local_prompts)], axis=1)

    own_grads = lax.psum_scatter(prompt_term(), "resp", scatter_dimension=0, tiled=True)
    for slot in range(local_prompts):
        segment = own_grads[:, slot * head_dim : (slot + 1) * head_dim]
        down_term, up_term = prompt_terms(
            prompt_hidden[slot], lowered_all[slot], segment, v_up[prompt_tenant[slot]]
        )
        down_terms.append(down_term)
        up_terms.append(up_term)
    per_prompt = []
    for slot in range(local_prompts):
        chosen_here = picked[slot]
        per_prompt.append(
            jnp.concatenate(
                [
                    (chosen_here * query_down_gradient).ravel(),
                    (chosen_here * value_down_gradient + down_terms[slot]).ravel(),
                    (chosen_here * query_up_gradient).ravel(),
                    (chosen_here * value_up_gradient + up_terms[slot]).ravel(),
                ]
            )
        )
    stacked = jnp.stack(per_prompt)
    tenant_onehot = (prompt_tenant[:, None] == jnp.arange(tenant_count)[None, :]).astype(
        jnp.float32
    )
    by_tenant = jnp.dot(tenant_onehot.T, stacked, precision=hidden_prompt)
    summed = lax.psum(by_tenant, ("prompt", "resp"))
    width = response_input.shape[1]
    first = width * rank
    second = 2 * width * rank
    third = second + rank * heads * head_dim
    grad_q_down = summed[:, :first].reshape(tenant_count, width, rank)
    grad_v_down = summed[:, first:second].reshape(tenant_count, width, rank)
    grad_q_up = summed[:, second:third].reshape(tenant_count, rank, heads * head_dim)
    grad_v_up = summed[:, third:].reshape(tenant_count, rank, head_dim)
    return (attn_out, grad_q_down, grad_q_up, grad_v_down, grad_v_up)


def solution(mesh):
    return jax.shard_map(
        per_device,
        mesh=mesh,
        in_specs=(
            P("prompt", "resp", None),
            P("prompt", "resp", None),
            P("prompt", "resp", None),
            P("prompt", "resp", None),
            P("prompt", "resp", None),
            P("prompt", "resp", None),
            P("prompt", "resp", None),
            P("prompt", "resp", None),
            P("prompt", "resp"),
            P("prompt", "resp"),
            P("prompt", "resp"),
            P("prompt"),
            P(),
            P(),
            P(),
            P(),
        ),
        out_specs=(P("prompt", "resp", None), P(), P(), P(), P()),
        check_vma=False,
    )
```

profile of v0, /device:TPU:1, one launch (start us, length us, event | category | flops | bytes accessed | tf_op | source)
XLA Modules:
  0.0 810.5 jit_solution(11151113947078540779)
XLA Ops:
  22.1 109.7 %all-reduce = (f32[2]{0:T(128)S(1)}, f32[2]{0:T(128)S(1)}) all-reduce(f32[2]{0:T(128)S(1)} %fusion.126, f32[2]{0:T(128)S(1)} %fusion.125), channel_id=1, replica_groups=mesh['prompt'=8,'resp'=32] {'resp'}, use_global_device_ids=true, to_apply=%region_4.5 | all-reduce | flops 4 | bytes 32 | tf_op jit(solution)/shard_map/psum | solution.py:79
  138.9 2.2 multiply_reduce_fusion
  142.7 4.2 fusion.4
  146.9 38.5 %all-gather.5.cloned.1.call-done = bf16[2,3072,128]{2,1,0:T(8,128)(2,1)} async-done(((bf16[2,96,128]{2,1,0:T(8,128)(2,1)}), bf16[2,3072,128]{2,1,0:T(8,128)(2,1)}) %all-gather.5.cloned.1.call-update) | async-done | bytes 1572880 | tf_op jit(solution)/shard_map/all_gather | solution.py:73
  185.4 4.9 multiply_reduce_fusion.1
  190.3 1.9 broadcast_multiply_fusion.1
  194.1 3.6 copy.45
  199.7 5.0 fusion.6
  206.5 2.2 copy.37
  208.7 2.3 reshape.110
  211.0 2.2 copy.39
  213.3 2.3 reshape.114
  217.0 232.5 %reduce-scatter.4.cloned.1.call-done = f32[96,256]{1,0:T(8,128)} async-done(((f32[3072,256]{1,0:T(8,128)}), f32[96,256]{1,0:T(8,128)}) %reduce-scatter.4.cloned.1.call-update) | async-done | bytes 98320
  454.3 2.2 copy.38
  456.5 2.3 reshape.111
  458.8 2.2 copy.40
  461.1 2.3 reshape.115
  463.8 6.3 fusion.11
  471.9 267.3 %all-reduce.3.cloned.1.call-done = f32[8,182272]{1,0:T(8,128)} async-done(((f32[8,182272]{1,0:T(8,128)}), f32[8,182272]{1,0:T(8,128)}) %all-reduce.3.cloned.1.call-update) | async-done | bytes 5832720 | tf_op jit(solution)/shard_map/psum | solution.py:199
  742.8 5.2 fusion.132
  748.0 15.6 %reshape.120 = f32[8,5120,16]{2,1,0:T(8,128)} reshape(f32[8,81920]{1,0:T(8,128)} %get-tuple-element.24) | data formatting | bytes 5242880 | tf_op jit(solution)/shard_map/reshape | solution.py:205
  763.6 12.3 %copy.43 = f32[8,5120,16]{1,2,0:T(8,128)} copy(f32[8,5120,16]{2,1,0:T(8,128)} %reshape.120) | data formatting | bytes 5242880
  775.9 15.6 %reshape.118 = f32[8,5120,16]{2,1,0:T(8,128)} reshape(f32[8,81920]{1,0:T(8,128)} %get-tuple-element.25) | data formatting | bytes 5242880 | tf_op jit(solution)/shard_map/reshape | solution.py:204
  791.5 12.4 %copy.41 = f32[8,5120,16]{1,2,0:T(8,128)} copy(f32[8,5120,16]{2,1,0:T(8,128)} %reshape.118) | data formatting | bytes 5242880
  (107 shorter events, 31.3 us)
Async XLA Ops:
  7.2 6.7 copy-start
  7.2 126.5 %copy-start.3 = (bf16[1,64,5120]{2,1,0:T(8,128)(2,1)S(1)}, bf16[1,64,5120]{2,1,0:T(8,128)(2,1)}, u32[]{:S(2)}) copy-start(bf16[1,64,5120]{2,1,0:T(8,128)(2,1)} %param.19) | copy-start | bytes 1966084
  7.2 127.7 %copy-start.9 = (bf16[1,64,1024]{2,1,0:T(8,128)(2,1)S(1)}, bf16[1,64,1024]{2,1,0:T(8,128)(2,1)}, u32[]{:S(2)}) copy-start(bf16[1,64,1024]{2,1,0:T(8,128)(2,1)} %param.20) | copy-start | bytes 393220
  7.2 129.5 %copy-start.6 = (bf16[1,64,1024]{2,1,0:T(8,128)(2,1)S(1)}, bf16[1,64,1024]{2,1,0:T(8,128)(2,1)}, u32[]{:S(2)}) copy-start(bf16[1,64,1024]{2,1,0:T(8,128)(2,1)} %param.23) | copy-start | bytes 393220
  7.2 131.7 %all-gather.3.cloned.1.call-start = ((), (), s32[]{:S(2)}) async-start(), calls=%async_computation.1 | async-start | bytes 1622016 | tf_op jit(solution)/shard_map/all_gather | solution.py:72
  7.9 177.4 %all-gather.5.cloned.1.call-start = ((), (), s32[]{:S(2)}) async-start(), calls=%async_computation.2 | async-start | bytes 1622016 | tf_op jit(solution)/shard_map/all_gather | solution.py:73
  13.9 123.9 %copy-start.12 = (bf16[1,64,128]{2,1,0:T(8,128)(2,1)S(1)}, bf16[1,64,128]{2,1,0:T(8,128)(2,1)}, u32[]{:S(2)}) copy-start(bf16[1,64,128]{2,1,0:T(8,128)(2,1)} %param.22) | copy-start | bytes 49156
  15.5 123.2 %copy-start.20 = (bf16[1,64,128]{2,1,0:T(8,128)(2,1)S(1)}, bf16[1,64,128]{2,1,0:T(8,128)(2,1)}, u32[]{:S(2)}) copy-start(bf16[1,64,128]{2,1,0:T(8,128)(2,1)} %param.21) | copy-start | bytes 49156
  19.6 429.8 %reduce-scatter.4.cloned.1.call-start = ((), (), s32[]{:S(2)}) async-start(), calls=%async_computation.4 | async-start | bytes 3244032
  19.7 122.8 %copy-start.13 = (s32[512]{0:T(512)}, s32[512]{0:T(512)S(1)}, u32[]{:S(2)}) copy-start(s32[512]{0:T(512)S(1)} %add_select_fusion) | copy-start | bytes 6148
  21.0 121.5 %copy-start.18 = (pred[64]{0:T(512)(128)(4,1)}, pred[64]{0:T(512)(128)(4,1)S(1)}, u32[]{:S(2)}) copy-start(pred[64]{0:T(512)(128)(4,1)S(1)} %iota_compare_fusion.2) | copy-start | bytes 196
  138.9 65.7 %copy-start.10 = (f32[512,64]{0,1:T(8,128)}, f32[512,64]{0,1:T(8,128)S(1)}, u32[]{:S(2)}) copy-start(f32[512,64]{0,1:T(8,128)S(1)} %get-tuple-element.41) | copy-start | bytes 393220
  185.4 4.9 copy-start.2
  197.7 1.7 copy-start.7
  197.7 1.8 copy-start.17
  197.7 1.9 copy-start.4
  197.7 541.4 %all-reduce.3.cloned.1.call-start = ((), (), s32[]{:S(2)}) async-start(), calls=%async_computation.3 | async-start | bytes 11665408 | tf_op jit(solution)/shard_map/psum | solution.py:199
  199.6 5.0 copy-start.14
  199.7 5.0 copy-start.19
  199.7 5.0 copy-start.21
  211.0 4.6 copy-start.11
  458.8 4.6 copy-start.8
  461.1 2.7 copy-start.15
  791.5 12.4 %copy-start.1 = (bf16[8,5120,16]{1,2,0:T(8,128)(2,1)S(1)}, bf16[8,5120,16]{1,2,0:T(8,128)(2,1)}, u32[]{:S(2)}) copy-start(bf16[8,5120,16]{1,2,0:T(8,128)(2,1)} %param.30) | copy-start | bytes 3932164
  (2 other events, 1.5 us)
Sparse Core Ops, SparseCore 0:
  11.5 88.3 all-gather.2
  103.9 81.4 all-gather.4
  197.9 251.5 reduce-scatter.3
  470.3 268.8 all-reduce.2
where the time goes:
time: 813 us; the launch traced here: 810 us
  waiting for transfers between devices  539 us (66%)
  blocking collectives  110 us (14%)
  local copies, waits for them, and re-layouts  91.5 us (11%)
  matrix products  37.3 us (5%)
  between operations  23.8 us (3%)
  other arithmetic  8.82 us (1%)
    psum x1, waiting for transfers between devices, per_device(): summed = lax.psum(by_tenant, ('prompt', 'resp'))  267 us
    unnamed x5, waiting for transfers between devices  233 us
    psum x1, blocking collectives, per_device(): sums, counts = lax.psum((picked * reward, picked), 'resp')  110 us
    all_gather x1, waiting for transfers between devices, per_device(): lax.all_gather(lifted_stack, 'resp', axis=1, tiled=True)  38.5 us
    unnamed x51, local copies, waits for them, and re-layouts  31.6 us
  transfers between devices with their start and end apart: 4, of which 3 were waited for; matrix products, arithmetic and copies ran while one was open for 5% of the time, Pallas kernels for 0%

commit v1 on v0

v1 whole, which is shorter than its diff:
```python
import functools

import jax
import jax.numpy as jnp
from jax import lax
from jax.experimental import pallas as pl
from jax.experimental.pallas import tpu as pltpu
from jax.sharding import PartitionSpec as P

MESH = pl.DeviceIdType.MESH
F32 = jnp.float32
BF16 = jnp.bfloat16
NX = 4
NZ = 8
SIDE = NX * NX
LOG2E = 1.4426950408889634


def dot_nn(a, b):
    return lax.dot_general(a, b, (((1,), (0,)), ((), ())), preferred_element_type=F32)


def dot_nt(a, b):
    return lax.dot_general(a, b, (((1,), (1,)), ((), ())), preferred_element_type=F32)


def dot_tn(a, b):
    return lax.dot_general(a, b, (((0,), (0,)), ((), ())), preferred_element_type=F32)


class Place:
    def __init__(self):
        r = lax.axis_index("resp")
        p = lax.axis_index("prompt")
        self.x = r // 8
        self.y = lax.rem(r // 2, 4)
        self.zh = lax.rem(r, 2)
        self.zl = p // 2
        self.c = lax.rem(p, 2)
        self.z = self.zh * 4 + self.zl
        self.p = self.x * 4 + self.y

    def plane(self, dx, dy):
        x = lax.rem(self.x + dx, 4)
        y = lax.rem(self.y + dy, 4)
        return {"resp": (x * 4 + y) * 2 + self.zh}, x * 4 + y

    def line(self, dz):
        z = lax.rem(self.z + dz, NZ)
        return {
            "prompt": lax.rem(z, 4) * 2 + self.c,
            "resp": self.p * 2 + z // 4,
        }, z

    def other_core(self):
        return {"prompt": self.zl * 2 + (1 - self.c)}

    def along(self, axis, d):
        return self.plane(d, 0)[0] if axis == 0 else self.plane(0, d)[0]


class Spread:
    def __init__(self, at, buf, axis, send, recv, base):
        self.at = at
        self.buf = buf
        self.axis = axis
        self.a = at.x if axis == 0 else at.y
        self.b = at.y if axis == 0 else at.x
        self.send = send
        self.recv = recv
        self.base = base
        self.sent = []

    def copy(self, src, dst, sem, device):
        return pltpu.make_async_remote_copy(
            src_ref=src,
            dst_ref=dst,
            send_sem=self.send.at[self.base + sem],
            recv_sem=self.recv.at[self.base + sem],
            device_id=device,
            device_id_type=MESH,
        )

    def push(self, ref, sem, device):
        c = self.copy(ref, ref, sem, device)
        c.start()
        self.sent.append(c)

    def take(self, ref, sem, device):
        self.copy(ref, ref, sem, device).wait_recv()

    def first(self):
        mine = self.buf.at[self.a, self.b]
        for d in (1, 3, 2):
            self.push(mine, d - 1, self.at.along(1 - self.axis, d))

    def second(self):
        for d in (1, 3, 2):
            self.take(
                self.buf.at[self.a, lax.rem(self.b + 4 - d, 4)],
                d - 1,
                self.at.along(1 - self.axis, d),
            )
        row = self.buf.at[self.a]
        self.push(row, 3, self.at.along(self.axis, 1))
        self.push(row, 4, self.at.along(self.axis, 3))

    def relay(self):
        low = lax.rem(self.a + 3, 4)
        high = lax.rem(self.a + 1, 4)
        self.take(self.buf.at[low], 3, self.at.along(self.axis, 1))
        self.push(self.buf.at[low, pl.ds(0, 2)], 5, self.at.along(self.axis, 1))
        self.take(self.buf.at[high], 4, self.at.along(self.axis, 3))
        self.push(self.buf.at[high, pl.ds(2, 2)], 6, self.at.along(self.axis, 3))

    def finish(self):
        far = lax.rem(self.a + 2, 4)
        self.take(self.buf.at[far, pl.ds(0, 2)], 5, self.at.along(self.axis, 1))
        self.take(self.buf.at[far, pl.ds(2, 2)], 6, self.at.along(self.axis, 3))

    def drain(self):
        for c in self.sent:
            c.wait_send()


SPREAD_SEMS = 7


def step_kernel(
    dims,
    ph_hbm, pk_ref, pv_ref, rh_hbm, rq_ref, rk_ref, rv_ref, cot_ref,
    rew_ref, rp_ref, rl_ref, pt_ref, qd_hbm, qu_ref, vd_hbm, vu_ref,
    attn_ref, gath,
    ph, rh, qd, vd,
    k_own, k_par, v_own, v_par,
    s_scr, e_scr, v_scr, m_scr, l_scr, o_scr, dq_scr,
    stat, stat_in,
    rsb, rsr, bs32, bs16, bz_in,
    g_send, g_in, zbuf, acc32, acc16, core_in, vterm,
    load_sem, sp_send, sp_recv, z_send, z_recv, st_send, st_recv,
    rs_send, rs_recv, bz_sem, g_ssem, g_rsem, zl_ssem, zl_rsem, c_sem, f_sem,
):
    (D, HD, HQ, R, T, PB, RL) = dims
    at = Place()
    rows = RL * HQ
    qtiles = (D + HQ * HD) // HD
    dtiles = D // HD
    per = qtiles // SIDE
    half_t = T // 2

    loads = [
        pltpu.make_async_copy(s, d, load_sem.at[i])
        for i, (s, d) in enumerate(((ph_hbm, ph), (vd_hbm, vd), (rh_hbm, rh), (qd_hbm, qd)))
    ]
    for c in loads:
        c.start()

    barrier = pltpu.get_barrier_semaphore()

    def greet_plane(k, _):
        pl.semaphore_signal(
            barrier, inc=1, device_id=at.plane(k // 4, lax.rem(k, 4))[0], device_id_type=MESH
        )
        return 0

    def greet_line(k, _):
        pl.semaphore_signal(barrier, inc=1, device_id=at.line(k)[0], device_id_type=MESH)
        return 0

    lax.fori_loop(1, SIDE, greet_plane, 0)
    lax.fori_loop(1, NZ, greet_line, 0)
    pl.semaphore_signal(barrier, inc=1, device_id=at.other_core(), device_id_type=MESH)

    for s in range(2):
        a, b = (at.x, at.y) if s == 0 else (at.y, at.x)
        k_own[s, a, b] = pk_ref[s]
        v_own[s, a, b, 0:PB, :] = pv_ref[s]
        v_own[s, a, b, PB : PB + R, :] = jnp.zeros((R, HD), BF16)
    rsb[...] = jnp.zeros(rsb.shape, BF16)
    for t in range(dtiles + 1, qtiles):
        for s in range(2):
            g_send[1, t // per, s, t % per] = jnp.zeros((R, HD), BF16)

    chosen = rp_ref[0, 0]
    length = rl_ref[0, 0]
    reward = rew_ref[0, 0]
    pick = [(chosen == s).astype(F32) for s in range(2)]
    ten = [pt_ref[0], pt_ref[1]]
    own_ten = jnp.where(chosen == 0, ten[0], ten[1])

    row8 = lax.broadcasted_iota(jnp.int32, (8, HD), 0)
    stat[0] = jnp.where(
        row8 == 0,
        reward * pick[0],
        jnp.where(
            row8 == 1,
            reward * pick[1],
            jnp.where(row8 == 2, pick[0], jnp.where(row8 == 3, pick[1], 0.0)),
        ),
    )

    pl.semaphore_wait(barrier, SIDE - 1 + NZ - 1 + 1)

    def spread(buf, s, i):
        return Spread(at, buf.at[s], s, sp_send, sp_recv, i * SPREAD_SEMS)

    ko = [spread(k_own, s, s) for s in range(2)]
    kp = [spread(k_par, s, 2 + s) for s in range(2)]
    vo = [spread(v_own, s, 4 + s) for s in range(2)]
    vp = [spread(v_par, s, 6 + s) for s in range(2)]
    partner = at.line(4)[0]

    def across(src, dst, s, i):
        a, b = (at.x, at.y) if s == 0 else (at.y, at.x)
        return pltpu.make_async_remote_copy(
            src_ref=src.at[s, a, b], dst_ref=dst.at[s, a, b],
            send_sem=z_send.at[i], recv_sem=z_recv.at[i],
            device_id=partner, device_id_type=MESH,
        )

    zk = [across(k_own, k_par, s, s) for s in range(2)]
    zv = [across(v_own, v_par, s, 2 + s) for s in range(2)]
    for s in range(2):
        zk[s].start()
    for s in range(2):
        ko[s].first()

    def stat_copy(step, d):
        i = step * 3 + d - 1
        device = partner if step == 2 else at.along(step, d)
        return pltpu.make_async_remote_copy(
            src_ref=stat.at[step], dst_ref=stat_in.at[i],
            send_sem=st_send.at[i], recv_sem=st_recv.at[i],
            device_id=device, device_id_type=MESH,
        )

    stat_copies = [[stat_copy(0, d) for d in (1, 2, 3)], [stat_copy(1, d) for d in (1, 2, 3)], [stat_copy(2, 1)]]

    def stat_start(step):
        for c in stat_copies[step]:
            c.start()

    def stat_sum(step):
        total = stat[step]
        for i, c in enumerate(stat_copies[step]):
            c.wait_recv()
            total = total + stat_in[step * 3 + i]
        stat[step + 1] = total

    stat_start(0)

    loads[0].wait()
    loads[1].wait()
    for s in range(2):
        a, b = (at.x, at.y) if s == 0 else (at.y, at.x)
        low = dot_nt(vd[ten[s]], ph[s]).astype(BF16)
        v_own[s, a, b, PB : PB + R, 0:PB] = low
    for s in range(2):
        ko[s].second()
    for s in range(2):
        zv[s].start()
    for s in range(2):
        vo[s].first()

    loads[2].wait()
    loads[3].wait()
    low_qv = dot_nt(jnp.concatenate([qd[own_ten], vd[own_ten]], axis=0), rh[...]).astype(BF16)
    low_q = low_qv[0:R]
    low_v = low_qv[R : 2 * R]
    q_up = qu_ref[own_ten]
    v_up = vu_ref[own_ten]
    queries = (rq_ref[...].astype(F32) + 2.0 * dot_tn(low_q, q_up)).astype(BF16)
    own_val = (rv_ref[...].astype(F32) + 2.0 * dot_tn(low_v, v_up)).astype(BF16)
    qh = jnp.concatenate([queries[:, h * HD : (h + 1) * HD] for h in range(HQ)], axis=0)
    rk = rk_ref[...]
    stat_sum(0)
    stat_start(1)

    for s in range(2):
        zk[s].wait_recv()
        kp[s].first()
    for s in range(2):
        ko[s].relay()
    for s in range(2):
        kp[s].second()
    for s in range(2):
        vo[s].second()

    factor = HD ** (-0.5) * LOG2E
    s_own = dot_nt(qh, rk)
    q_pos = lax.rem(lax.broadcasted_iota(jnp.int32, (rows, RL), 0), RL)
    k_pos = lax.broadcasted_iota(jnp.int32, (rows, RL), 1)
    allowed = (k_pos <= q_pos) & (k_pos < length)
    m_own = jnp.max(jnp.where(allowed, s_own, -1e30), axis=1, keepdims=True)

    stat_sum(1)
    stat_start(2)
    cols = 4 * PB
    for s in range(2):
        ko[s].finish()

    def scores(kbuf, base):
        def body(a, _):
            kc = kbuf[chosen, a].reshape(cols, HD)
            sc = dot_nt(qh, kc)
            s_scr[base + a] = sc
            top = sc[:, 0:HD]
            for j in range(1, cols // HD):
                top = jnp.maximum(top, sc[:, j * HD : (j + 1) * HD])
            m_scr[...] = jnp.maximum(m_scr[...], top)
            return 0

        lax.fori_loop(0, 4, body, 0)

    m_scr[...] = jnp.broadcast_to(m_own, (rows, HD))
    scores(k_own, 0)

    for s in range(2):
        zv[s].wait_recv()
        vp[s].first()
    for s in range(2):
        kp[s].relay()
    for s in range(2):
        vo[s].relay()
    for s in range(2):
        vp[s].second()
    for s in range(2):
        kp[s].finish()
    scores(k_par, 4)

    top = jnp.max(m_scr[...], axis=1, keepdims=True) * factor
    m_scr[...] = jnp.broadcast_to(top, (rows, HD))
    l_scr[...] = jnp.zeros((rows, HD), F32)

    def exps(c, _):
        sc = s_scr[c]
        mb = m_scr[...]
        part = l_scr[...]
        for j in range(cols // HD):
            ex = jnp.exp2(sc[:, j * HD : (j + 1) * HD] * factor - mb)
            part = part + ex
            e_scr[c, :, j * HD : (j + 1) * HD] = ex.astype(BF16)
        l_scr[...] = part
        return 0

    lax.fori_loop(0, 8, exps, 0)
    e_own = jnp.where(allowed, jnp.exp2(s_own * factor - top), 0.0)
    total = jnp.sum(l_scr[...], axis=1, keepdims=True) + jnp.sum(e_own, axis=1, keepdims=True)
    inv = 1.0 / total

    stat_sum(2)
    st = stat[3]
    mean = pick[0] * st[0:1] / jnp.maximum(st[2:3], 1.0) + pick[1] * st[1:2] / jnp.maximum(st[3:4], 1.0)
    weight = -(reward - mean) / RL
    live = (lax.broadcasted_iota(jnp.int32, (RL, HD), 0) < length).astype(F32) * weight
    ct = cot_ref[...].astype(F32)
    up = jnp.concatenate(
        [(ct[:, h * HD : (h + 1) * HD] * live).astype(BF16) for h in range(HQ)], axis=0
    )
    up32 = up.astype(F32)
    un = (up32 * inv).astype(BF16)
    uv = dot_nt(v_up, un).astype(BF16)
    e_own16 = e_own.astype(BF16)

    row_r = lax.broadcasted_iota(jnp.int32, (R, HD), 0)
    col_r = lax.broadcasted_iota(jnp.int32, (R, HD), 1)
    lift = jnp.concatenate(
        [2.0 * v_up.astype(F32), (row_r == col_r).astype(F32)], axis=1
    ).astype(BF16)

    def values(vbuf, base):
        def body(a, _):
            blk = vbuf[chosen, a]
            low_t = jnp.concatenate([blk[j, PB : PB + R, :] for j in range(4)], axis=1)
            ext = dot_tn(low_t, lift)
            for j in range(4):
                v_scr[base + a, j * PB : (j + 1) * PB, 0:HD] = (
                    blk[j, 0:PB, :].astype(F32) + ext[j * HD : j * HD + PB, 0:HD]
                ).astype(BF16)
                v_scr[base + a, j * PB : (j + 1) * PB, HD : 2 * HD] = ext[
                    j * HD : j * HD + PB, HD : 2 * HD
                ].astype(BF16)
            o_scr[...] += dot_nn(e_scr[base + a], v_scr[base + a])
            return 0

        lax.fori_loop(0, 4, body, 0)

    o_scr[:, 0:HD] = dot_nn(e_own16, own_val)
    o_scr[:, HD : 2 * HD] = jnp.zeros((rows, HD), F32)
    for s in range(2):
        vo[s].finish()
    values(v_own, 0)
    for s in range(2):
        vp[s].relay()
    for s in range(2):
        vp[s].finish()
    values(v_par, 4)

    attended = o_scr[:, 0:HD] * inv
    for h in range(HQ):
        attn_ref[:, h * HD : (h + 1) * HD] = attended[h * RL : (h + 1) * RL].astype(BF16)
    delta = jnp.sum(up32 * attended, axis=1, keepdims=True) * inv
    wl = o_scr[:, HD : HD + R].astype(BF16)
    vup_term = 2.0 * dot_tn(wl, un)

    ds_own = (e_own * (dot_nt(un, own_val) - delta)).astype(BF16)
    dq_scr[...] = dot_nn(ds_own, rk)
    m_scr[...] = jnp.broadcast_to(delta, (rows, HD))

    def backward(kbuf, base, z):
        def body(a, _):
            e16 = e_scr[base + a]
            dp = dot_nt(un, v_scr[base + a, :, 0:HD])
            db = m_scr[...]
            ds = jnp.concatenate(
                [
                    (
                        e16[:, j * HD : (j + 1) * HD].astype(F32)
                        * (dp[:, j * HD : (j + 1) * HD] - db)
                    ).astype(BF16)
                    for j in range(cols // HD)
                ],
                axis=1,
            )
            kc = kbuf[chosen, a].reshape(cols, HD)
            dq_scr[...] += dot_nn(ds, kc)
            back = dot_nn(uv, e16)
            for j in range(4):
                piece = back[:, j * PB : (j + 1) * PB]
                rsb[a * 4 + j, z, 0, :, 0:PB] = (piece * pick[0]).astype(BF16)
                rsb[j * 4 + a, z, 1, :, 0:PB] = (piece * pick[1]).astype(BF16)
            return 0

        lax.fori_loop(0, 4, body, 0)

    backward(k_own, 0, at.zh)
    backward(k_par, 4, 1 - at.zh)

    def plane_copy(src, dst, send, recv, k):
        device, p = at.plane(k // 4, lax.rem(k, 4))
        return pltpu.make_async_remote_copy(
            src_ref=src.at[p], dst_ref=dst.at[k], send_sem=send.at[k], recv_sem=recv.at[k],
            device_id=device, device_id_type=MESH,
        )

    def plane_start(src, dst, send, recv):
        def body(k, _):
            plane_copy(src, dst, send, recv, k).start()
            return 0

        lax.fori_loop(1, SIDE, body, 0)

    def plane_sum(src, dst, send, recv):
        def body(k, total):
            plane_copy(src, dst, send, recv, k).wait_recv()
            return total + dst[k].astype(F32)

        return lax.fori_loop(1, SIDE, body, src[at.p].astype(F32))

    def plane_drain(src, dst, send, recv):
        def body(k, _):
            plane_copy(src, dst, send, recv, k).wait_send()
            return 0

        lax.fori_loop(1, SIDE, body, 0)

    back_set = (rsb, rsr, rs_send, rs_recv)
    grad_set = [(g_send.at[i], g_in.at[i], g_ssem.at[i], g_rsem.at[i]) for i in range(2)]
    plane_start(*back_set)

    dq = (dq_scr[...] * (HD ** (-0.5))).astype(BF16)
    dq_wide = jnp.concatenate([dq[h * RL : (h + 1) * RL] for h in range(HQ)], axis=1)
    dov = dot_tn(e_own16, un).astype(BF16)
    qb = dot_nt(q_up, dq_wide).astype(BF16)
    vb = dot_nt(v_up, dov).astype(BF16)
    down = 2.0 * dot_nn(jnp.concatenate([qb, vb], axis=0), rh[...])
    q_term_up = 2.0 * dot_nn(low_q, dq_wide)
    vup_term = vup_term + 2.0 * dot_nn(low_v, dov)
    for t in range(qtiles):
        if t < dtiles:
            tile = down[0:R, t * HD : (t + 1) * HD]
        else:
            tile = q_term_up[:, (t - dtiles) * HD : (t - dtiles + 1) * HD]
        for s in range(2):
            g_send[0, t // per, s, t % per] = (tile * pick[s]).astype(BF16)
    vterm[...] = down[R : 2 * R]
    for s in range(2):
        g_send[1, dtiles // per, s, dtiles % per] = (vup_term * pick[s]).astype(BF16)
    plane_start(*grad_set[0])

    total_back = plane_sum(*back_set)
    bs32[...] = total_back
    bs16[...] = total_back.astype(BF16)
    bz = pltpu.make_async_remote_copy(
        src_ref=bs16.at[1 - at.zh], dst_ref=bz_in, send_sem=bz_sem.at[0], recv_sem=bz_sem.at[1],
        device_id=partner, device_id_type=MESH,
    )
    bz.start()

    r16 = lax.broadcasted_iota(jnp.int32, (R, HD), 0)
    owner = jnp.where(r16 < T, ten[0], ten[1])
    mask = (owner == lax.rem(r16, T)).astype(F32).astype(BF16)

    def line_copy(i, k, sender):
        device, _ = at.line(k)
        spot = zbuf.at[i, sender]
        return pltpu.make_async_remote_copy(
            src_ref=spot, dst_ref=spot, send_sem=zl_ssem.at[i, k], recv_sem=zl_rsem.at[i, k],
            device_id=device, device_id_type=MESH,
        )

    def line_start(i):
        total = plane_sum(*grad_set[i]).astype(BF16)
        zbuf[i, at.z, 0 : 2 * per] = total.reshape(2 * per, R, HD)
        zbuf[i, at.z, 2 * per] = mask

        def body(k, _):
            line_copy(i, k, at.z).start()
            return 0

        lax.fori_loop(1, NZ, body, 0)

    def core_copy(i):
        return pltpu.make_async_remote_copy(
            src_ref=acc16.at[i, 1 - at.c], dst_ref=core_in.at[i], send_sem=c_sem.at[i, 0],
            recv_sem=c_sem.at[i, 1], device_id=at.other_core(), device_id_type=MESH,
        )

    def line_sum(i):
        def waits(k, _):
            line_copy(i, k, lax.rem(at.z + NZ - k, NZ)).wait_recv()
            return 0

        lax.fori_loop(1, NZ, waits, 0)
        acc32[i] = jnp.zeros(acc32.shape[1:], F32)

        def body(z, _):
            tag = zbuf[i, z, 2 * per].astype(F32)
            for s in range(2):
                data = zbuf[i, z, s * per : (s + 1) * per].astype(F32)
                for t in range(T):
                    part = data * tag[s * T + t : s * T + t + 1][None]
                    acc32[i, t // half_t, t % half_t] += part
            return 0

        lax.fori_loop(0, NZ, body, 0)
        acc16[i] = acc32[i].astype(BF16)
        core_copy(i).start()

    streams = [
        [
            Spread(
                at, gath.at[i, at.c, h], h, sp_send, sp_recv, (8 + i * 2 + h) * SPREAD_SEMS
            )
            for h in range(2)
        ]
        for i in range(2)
    ]

    def gather_start(i):
        core_copy(i).wait_recv()
        final = (acc32[i, at.c] + core_in[i].astype(F32)).astype(BF16)
        for h in range(2):
            a, b = (at.x, at.y) if h == 0 else (at.y, at.x)
            gath[i, at.c, h, a, b] = final[2 * h : 2 * h + 2]
            streams[i][h].first()

    def final_copy(i, h, core):
        spot = gath.at[i, core, h]
        return pltpu.make_async_remote_copy(
            src_ref=spot, dst_ref=spot, send_sem=f_sem.at[i, h, 0], recv_sem=f_sem.at[i, h, 1],
            device_id=at.other_core(), device_id_type=MESH,
        )

    def gather_second(i):
        for h in range(2):
            streams[i][h].second()

    def gather_relay(i):
        for h in range(2):
            streams[i][h].relay()

    def gather_finish(i):
        for h in range(2):
            streams[i][h].finish()
            final_copy(i, h, at.c).start()

    line_start(0)

    bz.wait_recv()
    back = (bs32[at.zh] + bz_in[...].astype(F32)).astype(BF16)
    for s in range(2):
        term = 2.0 * dot_nn(back[s][:, 0:PB], ph[s]) + vterm[...] * pick[s]
        for t in range(dtiles):
            g_send[1, t // per, s, t % per] = term[:, t * HD : (t + 1) * HD].astype(BF16)
    plane_start(*grad_set[1])

    line_sum(0)
    gather_start(0)
    gather_second(0)
    line_start(1)
    gather_relay(0)
    line_sum(1)
    gather_start(1)
    gather_finish(0)
    gather_second(1)
    gather_relay(1)
    gather_finish(1)

    for c in zk + zv + [bz] + [c for step in stat_copies for c in step]:
        c.wait_send()
    for g in ko + kp + vo + vp + streams[0] + streams[1]:
        g.drain()
    plane_drain(*back_set)
    for i in range(2):
        plane_drain(*grad_set[i])

        def body(k, _):
            line_copy(i, k, at.z).wait_send()
            return 0

        lax.fori_loop(1, NZ, body, 0)
        core_copy(i).wait_send()
        for h in range(2):
            final_copy(i, h, at.c).wait_send()
            final_copy(i, h, 1 - at.c).wait_recv()


def widen_kernel(dims, gath, qd_ref, qu_ref, vd_ref, vu_ref):
    (D, HD, HQ, R, T, PB, RL) = dims
    t = pl.program_id(0)
    h = lax.rem(t, 4) // 2
    qtiles = (D + HQ * HD) // HD
    dtiles = D // HD
    per = qtiles // SIDE
    for i in range(2):
        for k in range(qtiles):
            p, j = k // per, k % per
            x, y = p // 4, p % 4
            a = jnp.where(h == 0, x, y)
            b = jnp.where(h == 0, y, x)
            if i == 1 and k > dtiles:
                continue
            tile = gath[i, 0, 0, a, b, 0, j].astype(F32)
            if k < dtiles:
                ref = qd_ref if i == 0 else vd_ref
                ref[0, :, k * HD : (k + 1) * HD] = tile
            else:
                ref = qu_ref if i == 0 else vu_ref
                ref[0, :, (k - dtiles) * HD : (k - dtiles + 1) * HD] = tile


def per_device(
    prompt_hidden, prompt_keys, prompt_values, resp_hidden, resp_queries, resp_keys, resp_values,
    cotangent, rewards, resp_prompt, resp_len, prompt_tenant, q_down, q_up, v_down, v_up,
):
    D = prompt_hidden.shape[2]
    PB = prompt_hidden.shape[1]
    HD = prompt_keys.shape[2]
    HQ = resp_queries.shape[2] // HD
    T, _, R = q_down.shape
    RL = resp_hidden.shape[1]
    dims = (D, HD, HQ, R, T, PB, RL)
    rows = RL * HQ
    per = (D + HQ * HD) // HD // SIDE
    cols = 4 * PB
    vmem = pl.BlockSpec(memory_space=pltpu.VMEM)
    smem = pl.BlockSpec(memory_space=pltpu.SMEM)
    hbm = pl.BlockSpec(memory_space=pl.ANY)
    dma = pltpu.SemaphoreType.DMA
    gath_shape = (2, 2, 2, 4, 4, 2, per, R, HD)
    attn, gath = pl.pallas_call(
        functools.partial(step_kernel, dims),
        name="step",
        out_shape=(
            jax.ShapeDtypeStruct((RL, HQ * HD), BF16),
            jax.ShapeDtypeStruct(gath_shape, BF16),
        ),
        in_specs=[hbm, vmem, vmem, hbm, vmem, vmem, vmem, vmem, smem, smem, smem, smem, hbm, vmem, hbm, vmem],
        out_specs=(vmem, vmem),
        scratch_shapes=[
            pltpu.VMEM((2, PB, D), BF16),
            pltpu.VMEM((RL, D), BF16),
            pltpu.VMEM((T, R, D), BF16),
            pltpu.VMEM((T, R, D), BF16),
            pltpu.VMEM((2, 4, 4, PB, HD), BF16),
            pltpu.VMEM((2, 4, 4, PB, HD), BF16),
            pltpu.VMEM((2, 4, 4, PB + R, HD), BF16),
            pltpu.VMEM((2, 4, 4, PB + R, HD), BF16),
            pltpu.VMEM((8, rows, cols), F32),
            pltpu.VMEM((8, rows, cols), BF16),
            pltpu.VMEM((8, cols, 2 * HD), BF16),
            pltpu.VMEM((rows, HD), F32),
            pltpu.VMEM((rows, HD), F32),
            pltpu.VMEM((rows, 2 * HD), F32),
            pltpu.VMEM((rows, HD), F32),
            pltpu.VMEM((4, 8, HD), F32),
            pltpu.VMEM((7, 8, HD), F32),
            pltpu.VMEM((SIDE, 2, 2, R, HD), BF16),
            pltpu.VMEM((SIDE, 2, 2, R, HD), BF16),
            pltpu.VMEM((2, 2, R, HD), F32),
            pltpu.VMEM((2, 2, R, HD), BF16),
            pltpu.VMEM((2, R, HD), BF16),
            pltpu.VMEM((2, SIDE, 2, per, R, HD), BF16),
            pltpu.VMEM((2, SIDE, 2, per, R, HD), BF16),
            pltpu.VMEM((2, NZ, 2 * per + 1, R, HD), BF16),
            pltpu.VMEM((2, 2, T // 2, per, R, HD), F32),
            pltpu.VMEM((2, 2, T // 2, per, R, HD), BF16),
            pltpu.VMEM((2, T // 2, per, R, HD), BF16),
            pltpu.VMEM((R, D), F32),
            dma((4,)),
            dma((12 * SPREAD_SEMS,)),
            dma((12 * SPREAD_SEMS,)),
            dma((4,)),
            dma((4,)),
            dma((7,)),
            dma((7,)),
            dma((SIDE,)),
            dma((SIDE,)),
            dma((2,)),
            dma((2, SIDE)),
            dma((2, SIDE)),
            dma((2, NZ)),
            dma((2, NZ)),
            dma((2, 2)),
            dma((2, 2, 2)),
        ],
        compiler_params=pltpu.CompilerParams(
            collective_id=0, has_side_effects=True, vmem_limit_bytes=56 * 2**20
        ),
    )(
        prompt_hidden, prompt_keys, prompt_values, resp_hidden[0], resp_queries[0], resp_keys[0],
        resp_values[0], cotangent[0], rewards, resp_prompt, resp_len, prompt_tenant,
        jnp.swapaxes(q_down, 1, 2), q_up, jnp.swapaxes(v_down, 1, 2), v_up,
    )

    def out_block(width):
        return pl.BlockSpec((1, R, width), lambda t: (t, 0, 0))

    qd_t, g_qu, vd_t, g_vu = pl.pallas_call(
        functools.partial(widen_kernel, dims),
        name="widen",
        grid=(T,),
        out_shape=(
            jax.ShapeDtypeStruct((T, R, D), F32),
            jax.ShapeDtypeStruct((T, R, HQ * HD), F32),
            jax.ShapeDtypeStruct((T, R, D), F32),
            jax.ShapeDtypeStruct((T, R, HD), F32),
        ),
        in_specs=[
            pl.BlockSpec(
                (2, 1, 1, 4, 4, 1, per, R, HD),
                lambda t: (0, t // 4, lax.rem(t, 4) // 2, 0, 0, lax.rem(t, 2), 0, 0, 0),
            )
        ],
        out_specs=(out_block(D), out_block(HQ * HD), out_block(D), out_block(HD)),
    )(gath)
    return (
        attn[None],
        jnp.swapaxes(qd_t, 1, 2),
        g_qu,
        jnp.swapaxes(vd_t, 1, 2),
        g_vu,
    )


def solution(mesh):
    rows = P("prompt", "resp", None)
    pair = P("prompt", "resp")
    return jax.shard_map(
        per_device,
        mesh=mesh,
        in_specs=(rows,) * 8 + (pair,) * 3 + (P("prompt"),) + (P(),) * 4,
        out_specs=(rows, P(), P(), P(), P()),
        check_vma=False,
    )
```

time: 813 us -> 107 us (0.13)
  waiting for transfers between devices: 539 us -> 0 us
  blocking collectives: 110 us -> 0 us
  Pallas kernels: 0 us -> 103 us
  local copies, waits for them, and re-layouts: 91.5 us -> 0.66 us
  matrix products: 37.3 us -> 0 us
  between operations: 23.8 us -> 2.59 us
  other arithmetic: 8.82 us -> 0 us
    psum x1 -> x0, waiting for transfers between devices: 267 us -> none  [per_device(): summed = lax.psum(by_tenant, ('prompt', 'resp'))]
    unnamed x5 -> x0, waiting for transfers between devices: 233 us -> none
    psum x1 -> x0, blocking collectives: 110 us -> none  [per_device(): sums, counts = lax.psum((picked * reward, picked), 'resp')]
    pallas_call x0 -> x2, Pallas kernels: none -> 103 us  [the longest x1 96.5 us: per_device(): pl.pallas_call(functools.partial(step_kernel, dims), name='step', out_sha...]
    reshape x10 -> x0, local copies, waits for them, and re-layouts: 42.1 us -> none  [the longest x1 15.6 us: per_device(): grad_v_down = summed[:, first:second].reshape(tenant_count, width, rank)]
    all_gather x2 -> x0, waiting for transfers between devices: 38.5 us -> none  [the longest x1 38.5 us: per_device(): lax.all_gather(lifted_stack, 'resp', axis=1, tiled=True)]
    dot_general x27 -> x0, matrix products: 37.3 us -> none  [the longest x1 6.31 us: per_device(): by_tenant = jnp.dot(tenant_onehot.T, stacked, precision=hidden_prompt)]
    unnamed x51 -> x3, local copies, waits for them, and re-layouts: 31.6 us -> 0.66 us
  transfers between devices with their start and end apart: 4 -> 0, of which waited for: 3 -> 0; matrix products, arithmetic and copies ran while one was open for 5% -> 0% of each run, Pallas kernels for 0% -> 0%
where the time goes in v1:
time: 107 us; the launch traced here: 106 us
  Pallas kernels  103 us (96%)
  between operations  2.59 us (2%)
    pallas_call x1, Pallas kernels, per_device(): pl.pallas_call(functools.partial(step_kernel, dims), name='step', out_sha...  96.5 us
    pallas_call x1, Pallas kernels, per_device(): pl.pallas_call(functools.partial(widen_kernel, dims), name='widen', grid=...  6.68 us

profile of v1, /device:TPU:1, one launch (start us, length us, event | category | flops | bytes accessed | tf_op | source)
XLA Modules:
  0.0 106.4 jit_solution(7591047023702720662)
XLA Ops:
  2.6 96.5 %step.1 = (bf16[64,1024]{1,0:T(8,128)(2,1)}, bf16[2,2,2,4,4,2,3,16,128]{8,7,6,5,4,3,2,1,0:T(8,128)(2,1)}) custom-call(bf16[2,96,5120]{2,1,0:T(8,128)(2,1)} %ph_hbm.1, bf16[2,96,128]{2,1,0:T(8,128)(2,1)} %pk_ref.1, bf16[2,96,128]{2,1,0:T(8,128)(2,1)} %pv_ref.1, bf16[64,5120]{1,0:T(8,128)(2,1)} %bitcast.12, bf16[64,1024]{1,0:T(8,128)(2,1)} %bitcast.13, ...), custom_call_target="tpu_custom_call" | custom-call | tf_op jit(solution)/shard_map/step/pallas_call | solution.py:672
  99.1 0.0 copy-start
  99.1 6.7 %widen.1 = (f32[8,16,5120]{2,1,0:T(8,128)}, f32[8,16,1024]{2,1,0:T(8,128)}, f32[8,16,5120]{2,1,0:T(8,128)}, f32[8,16,128]{2,1,0:T(8,128)}) custom-call(bf16[2,2,2,4,4,2,3,16,128]{8,7,6,5,4,3,2,1,0:T(8,128)(2,1)} %get-tuple-element.12.gath), custom_call_target="tpu_custom_call" | custom-call | tf_op jit(solution)/shard_map/widen/pallas_call | solution.py:740
  105.7 0.0 copy-done
  105.7 0.7 copy.25
Async XLA Ops:
  99.1 6.7 %copy-start = (bf16[64,1024]{1,0:T(8,128)(2,1)S(1)}, bf16[64,1024]{1,0:T(8,128)(2,1)}, u32[]{:S(2)}) copy-start(bf16[64,1024]{1,0:T(8,128)(2,1)} %get-tuple-element.11) | copy-start | bytes 393220

commit v2 on v1

v2 whole, which is shorter than its diff:
```python
import functools

import jax
import jax.numpy as jnp
from jax import lax
from jax.experimental import pallas as pl
from jax.experimental.pallas import tpu as pltpu
from jax.sharding import PartitionSpec as P

MESH = pl.DeviceIdType.MESH
F32 = jnp.float32
BF16 = jnp.bfloat16
NX = 4
NZ = 8
SIDE = NX * NX
LOG2E = 1.4426950408889634


def dot_nn(a, b):
    return lax.dot_general(a, b, (((1,), (0,)), ((), ())), preferred_element_type=F32)


def dot_nt(a, b):
    return lax.dot_general(a, b, (((1,), (1,)), ((), ())), preferred_element_type=F32)


def dot_tn(a, b):
    return lax.dot_general(a, b, (((0,), (0,)), ((), ())), preferred_element_type=F32)


class Place:
    def __init__(self):
        r = lax.axis_index("resp")
        p = lax.axis_index("prompt")
        self.x = r // 8
        self.y = lax.rem(r // 2, 4)
        self.zh = lax.rem(r, 2)
        self.zl = p // 2
        self.c = lax.rem(p, 2)
        self.z = self.zh * 4 + self.zl
        self.p = self.x * 4 + self.y

    def plane(self, dx, dy):
        x = lax.rem(self.x + dx, 4)
        y = lax.rem(self.y + dy, 4)
        return {"resp": (x * 4 + y) * 2 + self.zh}, x * 4 + y

    def line(self, dz):
        z = lax.rem(self.z + dz, NZ)
        return {
            "prompt": lax.rem(z, 4) * 2 + self.c,
            "resp": self.p * 2 + z // 4,
        }, z

    def other_core(self):
        return {"prompt": self.zl * 2 + (1 - self.c)}

    def along(self, axis, d):
        return self.plane(d, 0)[0] if axis == 0 else self.plane(0, d)[0]


class Spread:
    def __init__(self, at, buf, axis, send, recv, base, forward=None):
        self.at = at
        self.buf = buf
        self.axis = axis
        self.a = at.x if axis == 0 else at.y
        self.b = at.y if axis == 0 else at.x
        self.send = send
        self.recv = recv
        self.base = base
        self.sent = []
        self.forward = forward or (lambda ref, step: None)

    def copy(self, src, dst, sem, device):
        return pltpu.make_async_remote_copy(
            src_ref=src,
            dst_ref=dst,
            send_sem=self.send.at[self.base + sem],
            recv_sem=self.recv.at[self.base + sem],
            device_id=device,
            device_id_type=MESH,
        )

    def push(self, ref, sem, device):
        c = self.copy(ref, ref, sem, device)
        c.start()
        self.sent.append(c)

    def take(self, ref, sem, device):
        self.copy(ref, ref, sem, device).wait_recv()

    def first(self):
        mine = self.buf.at[self.a, self.b]
        for d in (1, 3, 2):
            self.push(mine, d - 1, self.at.along(1 - self.axis, d))

    def second(self):
        for d in (1, 3, 2):
            self.take(
                self.buf.at[self.a, lax.rem(self.b + 4 - d, 4)],
                d - 1,
                self.at.along(1 - self.axis, d),
            )
        row = self.buf.at[self.a]
        self.push(row, 3, self.at.along(self.axis, 1))
        self.push(row, 4, self.at.along(self.axis, 3))
        self.forward(row, 0)

    def relay(self):
        low = lax.rem(self.a + 3, 4)
        high = lax.rem(self.a + 1, 4)
        self.take(self.buf.at[low], 3, self.at.along(self.axis, 1))
        self.push(self.buf.at[low, pl.ds(0, 2)], 5, self.at.along(self.axis, 1))
        self.forward(self.buf.at[low], 1)
        self.take(self.buf.at[high], 4, self.at.along(self.axis, 3))
        self.push(self.buf.at[high, pl.ds(2, 2)], 6, self.at.along(self.axis, 3))
        self.forward(self.buf.at[high], 2)

    def finish(self):
        far = lax.rem(self.a + 2, 4)
        self.take(self.buf.at[far, pl.ds(0, 2)], 5, self.at.along(self.axis, 1))
        self.take(self.buf.at[far, pl.ds(2, 2)], 6, self.at.along(self.axis, 3))
        self.forward(self.buf.at[far], 3)

    def drain(self):
        for c in self.sent:
            c.wait_send()


SPREAD_SEMS = 7
HOLD_SEMS = 9


class Hold:
    def __init__(self, at, raw, sel, out, send, recv, base):
        self.at = at
        self.raw = raw
        self.sel = sel
        self.out = out
        self.send = send
        self.recv = recv
        self.base = base
        self.par = lax.rem(at.x + at.y, 2)
        self.sent = []

    def copy(self, src, dst, sem, device):
        return pltpu.make_async_remote_copy(
            src_ref=src,
            dst_ref=dst,
            send_sem=self.send.at[self.base + sem],
            recv_sem=self.recv.at[self.base + sem],
            device_id=device,
            device_id_type=MESH,
        )

    def spot(self, par, x, y):
        return par, par * (x // 2) + (1 - par) * (y // 2)

    def mine(self):
        return self.raw.at[self.spot(self.par, self.at.x, self.at.y)]

    def columns(self, x):
        return self.out.at[lax.rem(x, 2), x // 2, lax.rem(x, 2)]

    def rows(self, y):
        return self.out.at[1 - lax.rem(y, 2), :, lax.rem(y, 2), y // 2]

    def first(self):
        mine = self.mine()
        for d in (1, 3, 2):
            c = self.copy(mine, mine, d - 1, self.at.plane(d * self.par, d * (1 - self.par))[0])
            c.start()
            self.sent.append(c)

    def second(self, picks, own):
        at = self.at
        for d in (1, 3, 2):
            par = lax.rem(self.par + d, 2)
            x = lax.rem(at.x + (4 - d) * par, 4)
            y = lax.rem(at.y + (4 - d) * (1 - par), 4)
            spot = self.raw.at[self.spot(par, x, y)]
            self.copy(spot, spot, d - 1, at.along(0, d)).wait_recv()
        for d in (1, 3, 2):
            for axis in range(2):
                p = picks(axis, d)
                self.sel[axis, d - 1] = self.raw[axis, :, 0] * p[0] + self.raw[axis, :, 1] * p[1]
                target = self.columns(at.x) if axis == 0 else self.rows(at.y)
                c = self.copy(self.sel.at[axis, d - 1], target, 3 + axis * 3 + d - 1, at.along(axis, d))
                c.start()
                self.sent.append(c)
        chosen = [self.raw[axis, :, 0] * own[0] + self.raw[axis, :, 1] * own[1] for axis in range(2)]
        self.out[lax.rem(at.x, 2), at.x // 2, lax.rem(at.x, 2)] = chosen[0]
        for i in range(2):
            self.out[1 - lax.rem(at.y, 2), i, lax.rem(at.y, 2), at.y // 2] = chosen[1][i]

    def finish(self):
        at = self.at
        for d in (1, 3, 2):
            spot = self.columns(lax.rem(at.x + 4 - d, 4))
            self.copy(spot, spot, 3 + d - 1, at.along(0, d)).wait_recv()
            spot = self.rows(lax.rem(at.y + 4 - d, 4))
            self.copy(spot, spot, 6 + d - 1, at.along(1, d)).wait_recv()

    def drain(self):
        for c in self.sent:
            c.wait_send()


def step_kernel(
    dims,
    ph_hbm, pk_hbm, pv_hbm, rh_hbm, rq_hbm, rk_hbm, rv_hbm, cot_hbm,
    rew_ref, rp_ref, rl_ref, pt_ref, qd_hbm, qu_hbm, vd_hbm, vu_hbm,
    attn_ref, gath_hbm,
    gath, ph, rh, qd, vd, rq_ref, rk_ref, rv_ref, cot_ref, qu_ref, vu_ref,
    k_raw, v_raw, k_sel, v_sel, k_all, v_all,
    s_scr, e_scr, v_scr, m_scr, l_scr, o_scr, dq_scr,
    stat, stat_in,
    rsb, rsr, bs32, bs16, bz_in,
    g_send, g_in, zbuf, tags, acc32, acc16, core_in, vterm,
    load_sem, h_send, h_recv, sp_send, sp_recv, z_send, z_recv, st_send, st_recv,
    rs_send, rs_recv, bz_sem, g_ssem, g_rsem, zl_ssem, zl_rsem, tag_ssem, tag_rsem, c_sem, f_sem, out_sem,
):
    (D, HD, HQ, R, T, PB, RL) = dims
    at = Place()
    rows = RL * HQ
    qtiles = (D + HQ * HD) // HD
    dtiles = D // HD
    per = qtiles // SIDE
    half_t = T // 2

    barrier = pltpu.get_barrier_semaphore()

    def greet_plane(k, _):
        pl.semaphore_signal(
            barrier, inc=1, device_id=at.plane(k // 4, lax.rem(k, 4))[0], device_id_type=MESH
        )
        return 0

    def greet_line(k, _):
        pl.semaphore_signal(barrier, inc=1, device_id=at.line(k)[0], device_id_type=MESH)
        return 0

    lax.fori_loop(1, SIDE, greet_plane, 0)
    lax.fori_loop(1, NZ, greet_line, 0)
    pl.semaphore_signal(barrier, inc=1, device_id=at.other_core(), device_id_type=MESH)

    par = lax.rem(at.x + at.y, 2)
    place = par * (at.x // 2) + (1 - par) * (at.y // 2)
    loads = [
        pltpu.make_async_copy(s, d, load_sem.at[i])
        for i, (s, d) in enumerate(
            (
                (pk_hbm, k_raw.at[0, par, place]),
                (pv_hbm, v_raw.at[0, par, place, :, pl.ds(0, PB)]),
                (ph_hbm, ph),
                (vd_hbm, vd),
                (rh_hbm, rh),
                (qd_hbm, qd),
                (rq_hbm, rq_ref),
                (qu_hbm, qu_ref),
                (vu_hbm, vu_ref),
                (rk_hbm, rk_ref),
                (rv_hbm, rv_ref),
                (cot_hbm, cot_ref),
            )
        )
    ]
    for c in loads:
        c.start()

    for s in range(2):
        v_raw[0, par, place, s, PB : PB + R, :] = jnp.zeros((R, HD), BF16)
    rsb[...] = jnp.zeros(rsb.shape, BF16)
    for t in range(dtiles + 1, qtiles):
        for s in range(2):
            g_send[1, t // per, s, t % per] = jnp.zeros((R, HD), BF16)

    chosen = rp_ref[0, 0]
    length = rl_ref[0, 0]
    reward = rew_ref[0, 0]
    pick = [(chosen == s).astype(F32) for s in range(2)]
    ten = [pt_ref[0], pt_ref[1]]
    own_ten = jnp.where(chosen == 0, ten[0], ten[1])

    row8 = lax.broadcasted_iota(jnp.int32, (8, HD), 0)
    stat[0] = jnp.where(
        row8 == 0,
        reward * pick[0],
        jnp.where(
            row8 == 1,
            reward * pick[1],
            jnp.where(row8 == 2, pick[0], jnp.where(row8 == 3, pick[1], 0.0)),
        ),
    )

    loads[0].wait()
    pl.semaphore_wait(barrier, SIDE - 1 + NZ - 1 + 1)

    def hold(raw, sel, out, z, i):
        return Hold(at, raw.at[z], sel.at[z], out.at[z], h_send, h_recv, i * HOLD_SEMS)

    ko, kp = [hold(k_raw, k_sel, k_all, z, z) for z in range(2)]
    vo, vp = [hold(v_raw, v_sel, v_all, z, 2 + z) for z in range(2)]
    partner = at.line(4)[0]

    def across(raw, i):
        return pltpu.make_async_remote_copy(
            src_ref=raw.at[0, par, place], dst_ref=raw.at[1, par, place],
            send_sem=z_send.at[i], recv_sem=z_recv.at[i],
            device_id=partner, device_id_type=MESH,
        )

    zk = across(k_raw, 0)
    zv = across(v_raw, 1)
    zk.start()
    ko.first()

    def stat_copy(step, d):
        i = step * 3 + d - 1
        device = partner if step == 2 else at.along(step, d)
        return pltpu.make_async_remote_copy(
            src_ref=stat.at[step], dst_ref=stat_in.at[i],
            send_sem=st_send.at[i], recv_sem=st_recv.at[i],
            device_id=device, device_id_type=MESH,
        )

    def pick_copy(d):
        return pltpu.make_async_remote_copy(
            src_ref=stat.at[0], dst_ref=stat_in.at[6 + d],
            send_sem=st_send.at[6 + d], recv_sem=st_recv.at[6 + d],
            device_id=at.along(1, d), device_id_type=MESH,
        )

    stat_copies = [[stat_copy(0, d) for d in (1, 2, 3)], [stat_copy(1, d) for d in (1, 2, 3)], [stat_copy(2, 1)]]
    pick_copies = [pick_copy(d) for d in (1, 2, 3)]

    def stat_start(step):
        for c in stat_copies[step]:
            c.start()

    def stat_sum(step):
        total = stat[step]
        for i, c in enumerate(stat_copies[step]):
            c.wait_recv()
            total = total + stat_in[step * 3 + i]
        stat[step + 1] = total

    def picks(axis, d):
        tile = stat_in[(0 if axis == 0 else 7) + 3 - d].astype(BF16)
        return [tile[2 + s : 3 + s] for s in range(2)]

    own_pick = [stat[0].astype(BF16)[2 + s : 3 + s] for s in range(2)]

    stat_start(0)
    for c in pick_copies:
        c.start()
    for i in (1, 2, 3):
        loads[i].wait()
    for s in range(2):
        low = dot_nt(vd[ten[s]], ph[s]).astype(BF16)
        v_raw[0, par, place, s, PB : PB + R, 0:PB] = low

    vo.first()

    r16 = lax.broadcasted_iota(jnp.int32, (R, HD), 0)
    owner = jnp.where(r16 < T, ten[0], ten[1])
    mask = (owner == lax.rem(r16, T)).astype(F32).astype(BF16)

    tags[at.z] = mask

    def tag_copy(k, sender):
        spot = tags.at[sender]
        return pltpu.make_async_remote_copy(
            src_ref=spot, dst_ref=spot, send_sem=tag_ssem.at[k], recv_sem=tag_rsem.at[k],
            device_id=at.line(k)[0], device_id_type=MESH,
        )

    def tag_start(k, _):
        tag_copy(k, at.z).start()
        return 0

    def tag_wait(k, _):
        tag_copy(k, at.z).wait_send()
        tag_copy(k, lax.rem(at.z + NZ - k, NZ)).wait_recv()
        return 0

    for c in loads[4:]:
        c.wait()
    low_qv = dot_nt(jnp.concatenate([qd[own_ten], vd[own_ten]], axis=0), rh[...]).astype(BF16)
    low_q = low_qv[0:R]
    low_v = low_qv[R : 2 * R]
    q_up = qu_ref[own_ten]
    v_up = vu_ref[own_ten]
    queries = (rq_ref[...].astype(F32) + 2.0 * dot_tn(low_q, q_up)).astype(BF16)
    own_val = (rv_ref[...].astype(F32) + 2.0 * dot_tn(low_v, v_up)).astype(BF16)
    qh = jnp.concatenate([queries[:, h * HD : (h + 1) * HD] for h in range(HQ)], axis=0)
    rk = rk_ref[...]
    stat_sum(0)
    for c in pick_copies:
        c.wait_recv()
    ko.second(picks, own_pick)
    stat_start(1)
    vo.second(picks, own_pick)

    factor = HD ** (-0.5) * LOG2E
    s_own = dot_nt(qh, rk)
    q_pos = lax.rem(lax.broadcasted_iota(jnp.int32, (rows, RL), 0), RL)
    k_pos = lax.broadcasted_iota(jnp.int32, (rows, RL), 1)
    allowed = (k_pos <= q_pos) & (k_pos < length)
    m_own = jnp.max(jnp.where(allowed, s_own, -1e30), axis=1, keepdims=True)

    zk.wait_recv()
    kp.first()
    zv.start()
    lax.fori_loop(1, NZ, tag_start, 0)
    stat_sum(1)
    stat_start(2)
    ko.finish()

    cols = 4 * PB
    row_r = lax.broadcasted_iota(jnp.int32, (R, HD), 0)
    col_r = lax.broadcasted_iota(jnp.int32, (R, HD), 1)
    lift = jnp.concatenate(
        [2.0 * v_up.astype(F32), (row_r == col_r).astype(F32)], axis=1
    ).astype(BF16)

    def keys(c):
        return k_all[c // 4, (c % 4) // 2, c % 2].reshape(cols, HD)

    def low_rows(c):
        return jnp.concatenate(
            [v_all[c // 4, (c % 4) // 2, c % 2, j // 2, j % 2, PB : PB + R, :] for j in range(4)], axis=1
        )

    def scores(half, start):
        m_scr[...] = jnp.broadcast_to(start, (rows, HD))
        for c in range(4 * half, 4 * half + 4):
            sc = dot_nt(qh, keys(c))
            s_scr[c] = sc
            top = sc[:, 0:HD]
            for j in range(1, cols // HD):
                top = jnp.maximum(top, sc[:, j * HD : (j + 1) * HD])
            m_scr[...] = jnp.maximum(m_scr[...], top)
        top = jnp.max(m_scr[...], axis=1, keepdims=True) * factor
        m_scr[...] = jnp.broadcast_to(top, (rows, HD))
        return top

    def exps(half):
        l_scr[...] = jnp.zeros((rows, HD), F32)
        for c in range(4 * half, 4 * half + 4):
            sc = s_scr[c]
            mb = m_scr[...]
            part = l_scr[...]
            for j in range(cols // HD):
                ex = jnp.exp2(sc[:, j * HD : (j + 1) * HD] * factor - mb)
                part = part + ex
                e_scr[c, :, j * HD : (j + 1) * HD] = ex.astype(BF16)
            l_scr[...] = part
        return jnp.sum(l_scr[...], axis=1, keepdims=True)

    def values(half):
        for c in range(4 * half, 4 * half + 4):
            ext = dot_tn(low_rows(c), lift)
            blk = v_all[c // 4, (c % 4) // 2, c % 2, :, :, 0:PB, :].reshape(4, PB, HD)
            for j in range(4):
                v_scr[c, j * PB : (j + 1) * PB, 0:HD] = (
                    blk[j].astype(F32) + ext[j * HD : j * HD + PB, 0:HD]
                ).astype(BF16)
                v_scr[c, j * PB : (j + 1) * PB, HD : 2 * HD] = ext[
                    j * HD : j * HD + PB, HD : 2 * HD
                ].astype(BF16)
            o_scr[half] += dot_nn(e_scr[c], v_scr[c])

    top0 = scores(0, m_own)
    kp.second(picks, own_pick)
    l0 = exps(0)
    e_own = jnp.where(allowed, jnp.exp2(s_own * factor - top0), 0.0)
    e_own16 = e_own.astype(BF16)
    l0 = l0 + jnp.sum(e_own, axis=1, keepdims=True)
    zv.wait_recv()
    vp.first()
    o_scr[0, :, 0:HD] = dot_nn(e_own16, own_val)
    o_scr[0, :, HD : 2 * HD] = jnp.zeros((rows, HD), F32)
    o_scr[1] = jnp.zeros((rows, 2 * HD), F32)
    vo.finish()
    values(0)

    stat_sum(2)
    st = stat[3]
    mean = pick[0] * st[0:1] / jnp.maximum(st[2:3], 1.0) + pick[1] * st[1:2] / jnp.maximum(st[3:4], 1.0)
    weight = -(reward - mean) / RL
    live = (lax.broadcasted_iota(jnp.int32, (RL, HD), 0) < length).astype(F32) * weight
    ct = cot_ref[...].astype(F32)
    up = jnp.concatenate(
        [(ct[:, h * HD : (h + 1) * HD] * live).astype(BF16) for h in range(HQ)], axis=0
    )
    up32 = up.astype(F32)

    kp.finish()
    top1 = scores(1, jnp.full((rows, 1), -1e30, F32))
    vp.second(picks, own_pick)
    l1 = exps(1)
    top = jnp.maximum(top0, top1)
    share0 = jnp.exp2(top0 - top)
    share1 = jnp.exp2(top1 - top)
    inv = 1.0 / (share0 * l0 + share1 * l1)
    scale = [share0 * inv, share1 * inv]
    un = [(up32 * scale[h]).astype(BF16) for h in range(2)]

    for c in range(8):
        half = c // 4
        if c % 4 == 0:
            uv = dot_nt(v_up, un[half]).astype(BF16)
        x = (c % 2) * 2 + (c % 4) // 2
        back = dot_nn(uv, e_scr[c])
        z = at.zh if half == 0 else 1 - at.zh
        for j in range(4):
            y = (j % 2) * 2 + j // 2
            piece = back[:, j * PB : (j + 1) * PB]
            for s in range(2):
                rsb[x * 4 + y, z, s, :, 0:PB] = (piece * pick[s]).astype(BF16)

    def plane_copy(src, dst, send, recv, k):
        device, p = at.plane(k // 4, lax.rem(k, 4))
        return pltpu.make_async_remote_copy(
            src_ref=src.at[p], dst_ref=dst.at[k], send_sem=send.at[k], recv_sem=recv.at[k],
            device_id=device, device_id_type=MESH,
        )

    def plane_start(src, dst, send, recv):
        def body(k, _):
            plane_copy(src, dst, send, recv, k).start()
            return 0

        lax.fori_loop(1, SIDE, body, 0)

    def plane_sum(src, dst, send, recv):
        def body(k, total):
            plane_copy(src, dst, send, recv, k).wait_recv()
            return total + dst[k].astype(F32)

        return lax.fori_loop(1, SIDE, body, src[at.p].astype(F32))

    def plane_drain(src, dst, send, recv):
        def body(k, _):
            plane_copy(src, dst, send, recv, k).wait_send()
            return 0

        lax.fori_loop(1, SIDE, body, 0)

    back_set = (rsb, rsr, rs_send, rs_recv)
    grad_set = [(g_send.at[i], g_in.at[i], g_ssem.at[i], g_rsem.at[i]) for i in range(2)]
    plane_start(*back_set)

    dov = dot_tn(e_own16, un[0]).astype(BF16)
    vb = dot_nt(v_up, dov).astype(BF16)
    vterm[...] = 2.0 * dot_nn(vb, rh[...])
    total_back = plane_sum(*back_set)
    bs32[...] = total_back
    bs16[...] = total_back.astype(BF16)
    bz = pltpu.make_async_remote_copy(
        src_ref=bs16.at[1 - at.zh], dst_ref=bz_in, send_sem=bz_sem.at[0], recv_sem=bz_sem.at[1],
        device_id=partner, device_id_type=MESH,
    )
    bz.start()

    vp.finish()
    values(1)

    attended = o_scr[0, :, 0:HD] * scale[0] + o_scr[1, :, 0:HD] * scale[1]
    for h in range(HQ):
        attn_ref[:, h * HD : (h + 1) * HD] = attended[h * RL : (h + 1) * RL].astype(BF16)
    delta = jnp.sum(up32 * attended, axis=1, keepdims=True)

    ds_own = (e_own * (dot_nt(un[0], own_val) - delta * scale[0])).astype(BF16)
    dq_scr[...] = dot_nn(ds_own, rk)
    for c in range(8):
        half = c // 4
        if c % 4 == 0:
            m_scr[...] = jnp.broadcast_to(delta * scale[half], (rows, HD))
        e16 = e_scr[c]
        dp = dot_nt(un[half], v_scr[c, :, 0:HD])
        db = m_scr[...]
        ds = jnp.concatenate(
            [
                (
                    e16[:, j * HD : (j + 1) * HD].astype(F32)
                    * (dp[:, j * HD : (j + 1) * HD] - db)
                ).astype(BF16)
                for j in range(cols // HD)
            ],
            axis=1,
        )
        dq_scr[...] += dot_nn(ds, keys(c))

    dq = (dq_scr[...] * (HD ** (-0.5))).astype(BF16)
    dq_wide = jnp.concatenate([dq[h * RL : (h + 1) * RL] for h in range(HQ)], axis=1)
    qb = dot_nt(q_up, dq_wide).astype(BF16)
    down = 2.0 * dot_nn(qb, rh[...])
    q_term_up = 2.0 * dot_nn(low_q, dq_wide)
    for t in range(qtiles):
        if t < dtiles:
            tile = down[:, t * HD : (t + 1) * HD]
        else:
            tile = q_term_up[:, (t - dtiles) * HD : (t - dtiles + 1) * HD]
        for s in range(2):
            g_send[0, t // per, s, t % per] = (tile * pick[s]).astype(BF16)
    plane_start(*grad_set[0])

    vup_term = 2.0 * (
        dot_tn(o_scr[0, :, HD : HD + R].astype(BF16), un[0])
        + dot_tn(o_scr[1, :, HD : HD + R].astype(BF16), un[1])
        + dot_nn(low_v, dov)
    )
    for s in range(2):
        g_send[1, dtiles // per, s, dtiles % per] = (vup_term * pick[s]).astype(BF16)
    bz.wait_recv()
    back = (bs32[at.zh] + bz_in[...].astype(F32)).astype(BF16)
    for s in range(2):
        term = 2.0 * dot_nn(back[s][:, 0:PB], ph[s]) + vterm[...] * pick[s]
        for t in range(dtiles):
            g_send[1, t // per, s, t % per] = term[:, t * HD : (t + 1) * HD].astype(BF16)
    plane_start(*grad_set[1])

    def line_copy(i, k, sender):
        device, _ = at.line(k)
        spot = zbuf.at[i, sender]
        return pltpu.make_async_remote_copy(
            src_ref=spot, dst_ref=spot, send_sem=zl_ssem.at[i, k], recv_sem=zl_rsem.at[i, k],
            device_id=device, device_id_type=MESH,
        )

    def line_start(i):
        total = plane_sum(*grad_set[i]).astype(BF16)
        zbuf[i, at.z] = total.reshape(2 * per, R, HD)

        def body(k, _):
            line_copy(i, k, at.z).start()
            return 0

        lax.fori_loop(1, NZ, body, 0)

    def core_copy(i):
        return pltpu.make_async_remote_copy(
            src_ref=acc16.at[i, 1 - at.c], dst_ref=core_in.at[i], send_sem=c_sem.at[i, 0],
            recv_sem=c_sem.at[i, 1], device_id=at.other_core(), device_id_type=MESH,
        )

    def line_sum(i):
        def waits(k, _):
            line_copy(i, k, lax.rem(at.z + NZ - k, NZ)).wait_recv()
            return 0

        lax.fori_loop(1, NZ, waits, 0)
        acc32[i] = jnp.zeros(acc32.shape[1:], F32)

        def body(z, _):
            tag = tags[z].astype(F32)
            for s in range(2):
                data = zbuf[i, z, s * per : (s + 1) * per].astype(F32)
                for t in range(T):
                    part = data * tag[s * T + t : s * T + t + 1][None]
                    acc32[i, t // half_t, t % half_t] += part
            return 0

        lax.fori_loop(0, NZ, body, 0)
        acc16[i] = acc32[i].astype(BF16)
        core_copy(i).start()

    forwards = []

    def make_forward(i, h):
        def forward(ref, step):
            c = pltpu.make_async_remote_copy(
                src_ref=ref, dst_ref=ref, send_sem=f_sem.at[i, h, step, 0],
                recv_sem=f_sem.at[i, h, step, 1], device_id=at.other_core(), device_id_type=MESH,
            )
            c.start()
            forwards.append(c)

        return forward

    streams = [
        [
            Spread(
                at, gath.at[i, at.c, h], h, sp_send, sp_recv, (i * 2 + h) * SPREAD_SEMS,
                make_forward(i, h),
            )
            for h in range(2)
        ]
        for i in range(2)
    ]

    def gather_start(i):
        core_copy(i).wait_recv()
        final = (acc32[i, at.c] + core_in[i].astype(F32)).astype(BF16)
        for h in range(2):
            a, b = (at.x, at.y) if h == 0 else (at.y, at.x)
            gath[i, at.c, h, a, b] = final[2 * h : 2 * h + 2]
            streams[i][h].first()

    def gather_second(i):
        for h in range(2):
            streams[i][h].second()

    def gather_relay(i):
        for h in range(2):
            streams[i][h].relay()

    def gather_finish(i):
        for h in range(2):
            streams[i][h].finish()

    def out_copy(i):
        return pltpu.make_async_copy(gath.at[i], gath_hbm.at[i], out_sem.at[i])

    def gather_out(i):
        for h in range(2):
            g = streams[i][h]
            for step, d in enumerate((0, 3, 1, 2)):
                row = gath.at[i, 1 - at.c, h, lax.rem(g.a + d, 4)]
                pltpu.make_async_remote_copy(
                    src_ref=row, dst_ref=row, send_sem=f_sem.at[i, h, step, 0],
                    recv_sem=f_sem.at[i, h, step, 1], device_id=at.other_core(),
                    device_id_type=MESH,
                ).wait_recv()
        out_copy(i).start()

    lax.fori_loop(1, NZ, tag_wait, 0)
    line_start(0)
    line_start(1)
    line_sum(0)
    line_sum(1)
    gather_start(0)
    gather_start(1)
    gather_second(0)
    gather_second(1)
    gather_relay(0)
    gather_relay(1)
    gather_finish(0)
    gather_finish(1)
    gather_out(0)
    gather_out(1)

    for c in [zk, zv, bz] + pick_copies + [c for step in stat_copies for c in step] + forwards:
        c.wait_send()
    for g in [ko, kp, vo, vp] + streams[0] + streams[1]:
        g.drain()
    plane_drain(*back_set)
    for i in range(2):
        plane_drain(*grad_set[i])

        def body(k, _):
            line_copy(i, k, at.z).wait_send()
            return 0

        lax.fori_loop(1, NZ, body, 0)
        core_copy(i).wait_send()
    for i in range(2):
        out_copy(i).wait()


def widen_kernel(
    dims, gath_hbm, attn_hbm, attn_out, qd_out, qu_out, vd_out, vu_out,
    gath, qd, qu, vd, vu, in_sem, out_sem, attn_sem,
):
    (D, HD, HQ, R, T, PB, RL) = dims
    qtiles = (D + HQ * HD) // HD
    dtiles = D // HD
    per = qtiles // SIDE
    attn = pltpu.make_async_copy(attn_hbm, attn_out, attn_sem)
    parts = [(i, c, h) for c in range(2) for h in range(2) for i in range(2)]
    loads = [
        pltpu.make_async_copy(gath_hbm.at[i, c, h], gath.at[i, c, h], in_sem.at[k])
        for k, (i, c, h) in enumerate(parts)
    ]
    for load in loads:
        load.start()
    attn.start()
    stores = []
    for k, (i, c, h) in enumerate(parts):
        loads[k].wait()
        down, up = (qd, qu) if i == 0 else (vd, vu)
        down_out, up_out = (qd_out, qu_out) if i == 0 else (vd_out, vu_out)
        first = c * 4 + h * 2
        for t in range(qtiles):
            if i == 1 and t > dtiles:
                continue
            p, j = t // per, t % per
            a, b = (p // 4, p % 4) if h == 0 else (p % 4, p // 4)
            tile = gath[i, c, h, a, b, :, j].astype(F32)
            if t < dtiles:
                down[first : first + 2, :, t * HD : (t + 1) * HD] = tile
            else:
                up[first : first + 2, :, (t - dtiles) * HD : (t - dtiles + 1) * HD] = tile
        pair = pl.ds(first, 2)
        for n, (src, dst) in enumerate(((down, down_out), (up, up_out))):
            store = pltpu.make_async_copy(src.at[pair], dst.at[pair], out_sem.at[2 * k + n])
            store.start()
            stores.append(store)
    for store in stores:
        store.wait()
    attn.wait()


def per_device(
    prompt_hidden, prompt_keys, prompt_values, resp_hidden, resp_queries, resp_keys, resp_values,
    cotangent, rewards, resp_prompt, resp_len, prompt_tenant, q_down, q_up, v_down, v_up,
):
    D = prompt_hidden.shape[2]
    PB = prompt_hidden.shape[1]
    HD = prompt_keys.shape[2]
    HQ = resp_queries.shape[2] // HD
    T, _, R = q_down.shape
    RL = resp_hidden.shape[1]
    dims = (D, HD, HQ, R, T, PB, RL)
    rows = RL * HQ
    per = (D + HQ * HD) // HD // SIDE
    cols = 4 * PB
    vmem = pl.BlockSpec(memory_space=pltpu.VMEM)
    smem = pl.BlockSpec(memory_space=pltpu.SMEM)
    hbm = pl.BlockSpec(memory_space=pl.ANY)
    dma = pltpu.SemaphoreType.DMA
    gath_shape = (2, 2, 2, 4, 4, 2, per, R, HD)
    attn, gath = pl.pallas_call(
        functools.partial(step_kernel, dims),
        name="step",
        out_shape=(
            jax.ShapeDtypeStruct((RL, HQ * HD), BF16),
            jax.ShapeDtypeStruct(gath_shape, BF16),
        ),
        in_specs=[hbm] * 8 + [smem] * 4 + [hbm] * 4,
        out_specs=(vmem, hbm),
        scratch_shapes=[
            pltpu.VMEM(gath_shape, BF16),
            pltpu.VMEM((2, PB, D), BF16),
            pltpu.VMEM((RL, D), BF16),
            pltpu.VMEM((T, R, D), BF16),
            pltpu.VMEM((T, R, D), BF16),
            pltpu.VMEM((RL, HQ * HD), BF16),
            pltpu.VMEM((RL, HD), BF16),
            pltpu.VMEM((RL, HD), BF16),
            pltpu.VMEM((RL, HQ * HD), BF16),
            pltpu.VMEM((T, R, HQ * HD), BF16),
            pltpu.VMEM((T, R, HD), BF16),
            pltpu.VMEM((2, 2, 2, 2, PB, HD), BF16),
            pltpu.VMEM((2, 2, 2, 2, PB + R, HD), BF16),
            pltpu.VMEM((2, 2, 3, 2, PB, HD), BF16),
            pltpu.VMEM((2, 2, 3, 2, PB + R, HD), BF16),
            pltpu.VMEM((2, 2, 2, 2, 2, PB, HD), BF16),
            pltpu.VMEM((2, 2, 2, 2, 2, PB + R, HD), BF16),
            pltpu.VMEM((8, rows, cols), F32),
            pltpu.VMEM((8, rows, cols), BF16),
            pltpu.VMEM((8, cols, 2 * HD), BF16),
            pltpu.VMEM((rows, HD), F32),
            pltpu.VMEM((rows, HD), F32),
            pltpu.VMEM((2, rows, 2 * HD), F32),
            pltpu.VMEM((rows, HD), F32),
            pltpu.VMEM((4, 8, HD), F32),
            pltpu.VMEM((10, 8, HD), F32),
            pltpu.VMEM((SIDE, 2, 2, R, HD), BF16),
            pltpu.VMEM((SIDE, 2, 2, R, HD), BF16),
            pltpu.VMEM((2, 2, R, HD), F32),
            pltpu.VMEM((2, 2, R, HD), BF16),
            pltpu.VMEM((2, R, HD), BF16),
            pltpu.VMEM((2, SIDE, 2, per, R, HD), BF16),
            pltpu.VMEM((2, SIDE, 2, per, R, HD), BF16),
            pltpu.VMEM((2, NZ, 2 * per, R, HD), BF16),
            pltpu.VMEM((NZ, R, HD), BF16),
            pltpu.VMEM((2, 2, T // 2, per, R, HD), F32),
            pltpu.VMEM((2, 2, T // 2, per, R, HD), BF16),
            pltpu.VMEM((2, T // 2, per, R, HD), BF16),
            pltpu.VMEM((R, D), F32),
            dma((12,)),
            dma((4 * HOLD_SEMS,)),
            dma((4 * HOLD_SEMS,)),
            dma((4 * SPREAD_SEMS,)),
            dma((4 * SPREAD_SEMS,)),
            dma((2,)),
            dma((2,)),
            dma((10,)),
            dma((10,)),
            dma((SIDE,)),
            dma((SIDE,)),
            dma((2,)),
            dma((2, SIDE)),
            dma((2, SIDE)),
            dma((2, NZ)),
            dma((2, NZ)),
            dma((NZ,)),
            dma((NZ,)),
            dma((2, 2)),
            dma((2, 2, 4, 2)),
            dma((2,)),
        ],
        compiler_params=pltpu.CompilerParams(
            collective_id=0, has_side_effects=True, vmem_limit_bytes=60 * 2**20
        ),
    )(
        prompt_hidden, prompt_keys, prompt_values, resp_hidden[0], resp_queries[0], resp_keys[0],
        resp_values[0], cotangent[0], rewards, resp_prompt, resp_len, prompt_tenant,
        jnp.swapaxes(q_down, 1, 2), q_up, jnp.swapaxes(v_down, 1, 2), v_up,
    )

    shapes = ((T, R, D), (T, R, HQ * HD), (T, R, D), (T, R, HD))
    attn, qd_t, g_qu, vd_t, g_vu = pl.pallas_call(
        functools.partial(widen_kernel, dims),
        name="widen",
        out_shape=(jax.ShapeDtypeStruct((RL, HQ * HD), BF16),)
        + tuple(jax.ShapeDtypeStruct(x, F32) for x in shapes),
        in_specs=[hbm, hbm],
        out_specs=(hbm,) * 5,
        scratch_shapes=[pltpu.VMEM(gath_shape, BF16)]
        + [pltpu.VMEM(x, F32) for x in shapes]
        + [dma((8,)), dma((16,)), dma],
        compiler_params=pltpu.CompilerParams(vmem_limit_bytes=60 * 2**20),
    )(gath, attn)
    return (
        attn[None],
        jnp.swapaxes(qd_t, 1, 2),
        g_qu,
        jnp.swapaxes(vd_t, 1, 2),
        g_vu,
    )


def solution(mesh):
    rows = P("prompt", "resp", None)
    pair = P("prompt", "resp")
    return jax.shard_map(
        per_device,
        mesh=mesh,
        in_specs=(rows,) * 8 + (pair,) * 3 + (P("prompt"),) + (P(),) * 4,
        out_specs=(rows, P(), P(), P(), P()),
        check_vma=False,
    )
```

time: 107 us -> 88.4 us (0.83)
  Pallas kernels: 103 us -> 85.7 us
    pallas_call x1, Pallas kernels: 96.5 us -> 80.4 us  [per_device(): pl.pallas_call(functools.partial(step_kernel, dims), name='step', out_sha...]
    pallas_call x1, Pallas kernels: 6.68 us -> 5.31 us  [per_device(): pl.pallas_call(functools.partial(widen_kernel, dims), name='widen', out_s...]
where the time goes in v2:
time: 88.4 us; the launch traced here: 88.3 us
  Pallas kernels  85.7 us (97%)
  between operations  2.58 us (3%)
    pallas_call x1, Pallas kernels, per_device(): pl.pallas_call(functools.partial(step_kernel, dims), name='step', out_sha...  80.4 us
    pallas_call x1, Pallas kernels, per_device(): pl.pallas_call(functools.partial(widen_kernel, dims), name='widen', out_s...  5.31 us

profile of v2, /device:TPU:1, one launch (start us, length us, event | category | flops | bytes accessed | tf_op | source)
XLA Modules:
  0.0 88.3 jit_solution(8947074361172535853)
XLA Ops:
  2.6 80.4 %step.1 = (bf16[64,1024]{1,0:T(8,128)(2,1)}, bf16[2,2,2,4,4,2,3,16,128]{8,7,6,5,4,3,2,1,0:T(8,128)(2,1)}) custom-call(bf16[2,96,5120]{2,1,0:T(8,128)(2,1)} %ph_hbm.1, bf16[2,96,128]{2,1,0:T(8,128)(2,1)} %pk_hbm.1, bf16[2,96,128]{2,1,0:T(8,128)(2,1)} %pv_hbm.1, bf16[64,5120]{1,0:T(8,128)(2,1)} %bitcast.12, bf16[64,1024]{1,0:T(8,128)(2,1)} %bitcast.13, ...), custom_call_target="tpu_custom_call" | custom-call | tf_op jit(solution)/shard_map/step/pallas_call | solution.py:826
  83.0 5.3 %widen.1 = (bf16[64,1024]{1,0:T(8,128)(2,1)}, f32[8,16,5120]{2,1,0:T(8,128)}, f32[8,16,1024]{2,1,0:T(8,128)}, f32[8,16,5120]{2,1,0:T(8,128)}, f32[8,16,128]{2,1,0:T(8,128)}) custom-call(bf16[2,2,2,4,4,2,3,16,128]{8,7,6,5,4,3,2,1,0:T(8,128)(2,1)} %get-tuple-element.12.gath_hbm, bf16[64,1024]{1,0:T(8,128)(2,1)} %get-tuple-element.13.attn_hbm), custom_call_target="tpu_custom_call" | custom-call | tf_op jit(solution)/shard_map/widen/pallas_call | solution.py:907

commit v3 on v2

--- a/solution.py
+++ b/solution.py
@@ -211,15 +211,15 @@
     dims,
     ph_hbm, pk_hbm, pv_hbm, rh_hbm, rq_hbm, rk_hbm, rv_hbm, cot_hbm,
     rew_ref, rp_ref, rl_ref, pt_ref, qd_hbm, qu_hbm, vd_hbm, vu_hbm,
-    attn_ref, gath_hbm,
-    gath, ph, rh, qd, vd, rq_ref, rk_ref, rv_ref, cot_ref, qu_ref, vu_ref,
+    attn_ref, gath,
+    ph, rh, qd, vd, rq_ref, rk_ref, rv_ref, cot_ref, qu_ref, vu_ref,
     k_raw, v_raw, k_sel, v_sel, k_all, v_all,
     s_scr, e_scr, v_scr, m_scr, l_scr, o_scr, dq_scr,
     stat, stat_in,
     rsb, rsr, bs32, bs16, bz_in,
     g_send, g_in, zbuf, tags, acc32, acc16, core_in, vterm,
     load_sem, h_send, h_recv, sp_send, sp_recv, z_send, z_recv, st_send, st_recv,
-    rs_send, rs_recv, bz_sem, g_ssem, g_rsem, zl_ssem, zl_rsem, tag_ssem, tag_rsem, c_sem, f_sem, out_sem,
+    rs_send, rs_recv, bz_sem, g_ssem, g_rsem, zl_ssem, zl_rsem, tag_ssem, tag_rsem, c_sem, f_sem,
 ):
     (D, HD, HQ, R, T, PB, RL) = dims
     at = Place()
@@ -362,6 +362,7 @@
         v_raw[0, par, place, s, PB : PB + R, 0:PB] = low
 
     vo.first()
+    zv.start()
 
     r16 = lax.broadcasted_iota(jnp.int32, (R, HD), 0)
     owner = jnp.where(r16 < T, ten[0], ten[1])
@@ -412,7 +413,6 @@
 
     zk.wait_recv()
     kp.first()
-    zv.start()
     lax.fori_loop(1, NZ, tag_start, 0)
     stat_sum(1)
     stat_start(2)
@@ -556,6 +556,14 @@
     dov = dot_tn(e_own16, un[0]).astype(BF16)
     vb = dot_nt(v_up, dov).astype(BF16)
     vterm[...] = 2.0 * dot_nn(vb, rh[...])
+    vp.finish()
+    values(1)
+
+    attended = o_scr[0, :, 0:HD] * scale[0] + o_scr[1, :, 0:HD] * scale[1]
+    for h in range(HQ):
+        attn_ref[:, h * HD : (h + 1) * HD] = attended[h * RL : (h + 1) * RL].astype(BF16)
+    delta = jnp.sum(up32 * attended, axis=1, keepdims=True)
+
     total_back = plane_sum(*back_set)
     bs32[...] = total_back
     bs16[...] = total_back.astype(BF16)
@@ -564,14 +572,6 @@
         device_id=partner, device_id_type=MESH,
     )
     bz.start()
-
-    vp.finish()
-    values(1)
-
-    attended = o_scr[0, :, 0:HD] * scale[0] + o_scr[1, :, 0:HD] * scale[1]
-    for h in range(HQ):
-        attn_ref[:, h * HD : (h + 1) * HD] = attended[h * RL : (h + 1) * RL].astype(BF16)
-    delta = jnp.sum(up32 * attended, axis=1, keepdims=True)
 
     ds_own = (e_own * (dot_nt(un[0], own_val) - delta * scale[0])).astype(BF16)
     dq_scr[...] = dot_nn(ds_own, rk)
@@ -653,19 +653,15 @@
             return 0
 
         lax.fori_loop(1, NZ, waits, 0)
-        acc32[i] = jnp.zeros(acc32.shape[1:], F32)
-
-        def body(z, _):
-            tag = tags[z].astype(F32)
-            for s in range(2):
-                data = zbuf[i, z, s * per : (s + 1) * per].astype(F32)
-                for t in range(T):
-                    part = data * tag[s * T + t : s * T + t + 1][None]
-                    acc32[i, t // half_t, t % half_t] += part
-            return 0
-
-        lax.fori_loop(0, NZ, body, 0)
-        acc16[i] = acc32[i].astype(BF16)
+        tag = [tags[z].astype(F32) for z in range(NZ)]
+        for j in range(per):
+            data = [[zbuf[i, z, n * per + j].astype(F32) for n in range(2)] for z in range(NZ)]
+            for t in range(T):
+                part = sum(
+                    data[z][n] * tag[z][n * T + t : n * T + t + 1] for z in range(NZ) for n in range(2)
+                )
+                acc32[i, t // half_t, t % half_t, j] = part
+                acc16[i, t // half_t, t % half_t, j] = part.astype(BF16)
         core_copy(i).start()
 
     forwards = []
@@ -712,9 +708,6 @@
         for h in range(2):
             streams[i][h].finish()
 
-    def out_copy(i):
-        return pltpu.make_async_copy(gath.at[i], gath_hbm.at[i], out_sem.at[i])
-
     def gather_out(i):
         for h in range(2):
             g = streams[i][h]
@@ -725,7 +718,6 @@
                     recv_sem=f_sem.at[i, h, step, 1], device_id=at.other_core(),
                     device_id_type=MESH,
                 ).wait_recv()
-        out_copy(i).start()
 
     lax.fori_loop(1, NZ, tag_wait, 0)
     line_start(0)
@@ -757,30 +749,21 @@
 
         lax.fori_loop(1, NZ, body, 0)
         core_copy(i).wait_send()
-    for i in range(2):
-        out_copy(i).wait()
 
 
 def widen_kernel(
-    dims, gath_hbm, attn_hbm, attn_out, qd_out, qu_out, vd_out, vu_out,
-    gath, qd, qu, vd, vu, in_sem, out_sem, attn_sem,
+    dims, gath, attn_in, attn_out, qd_out, qu_out, vd_out, vu_out,
+    qd, qu, vd, vu, out_sem, attn_sem,
 ):
     (D, HD, HQ, R, T, PB, RL) = dims
     qtiles = (D + HQ * HD) // HD
     dtiles = D // HD
     per = qtiles // SIDE
-    attn = pltpu.make_async_copy(attn_hbm, attn_out, attn_sem)
+    attn = pltpu.make_async_copy(attn_in, attn_out, attn_sem)
     parts = [(i, c, h) for c in range(2) for h in range(2) for i in range(2)]
-    loads = [
-        pltpu.make_async_copy(gath_hbm.at[i, c, h], gath.at[i, c, h], in_sem.at[k])
-        for k, (i, c, h) in enumerate(parts)
-    ]
-    for load in loads:
-        load.start()
     attn.start()
     stores = []
     for k, (i, c, h) in enumerate(parts):
-        loads[k].wait()
         down, up = (qd, qu) if i == 0 else (vd, vu)
         down_out, up_out = (qd_out, qu_out) if i == 0 else (vd_out, vu_out)
         first = c * 4 + h * 2
@@ -827,13 +810,12 @@
         functools.partial(step_kernel, dims),
         name="step",
         out_shape=(
-            jax.ShapeDtypeStruct((RL, HQ * HD), BF16),
-            jax.ShapeDtypeStruct(gath_shape, BF16),
+            pltpu.VMEM((RL, HQ * HD), BF16),
+            pltpu.VMEM(gath_shape, BF16),
         ),
         in_specs=[hbm] * 8 + [smem] * 4 + [hbm] * 4,
-        out_specs=(vmem, hbm),
+        out_specs=(vmem, vmem),
         scratch_shapes=[
-            pltpu.VMEM(gath_shape, BF16),
             pltpu.VMEM((2, PB, D), BF16),
             pltpu.VMEM((RL, D), BF16),
             pltpu.VMEM((T, R, D), BF16),
@@ -892,10 +874,9 @@
             dma((NZ,)),
             dma((2, 2)),
             dma((2, 2, 4, 2)),
-            dma((2,)),
         ],
         compiler_params=pltpu.CompilerParams(
-            collective_id=0, has_side_effects=True, vmem_limit_bytes=60 * 2**20
+            collective_id=0, has_side_effects=True, vmem_limit_bytes=58 * 2**20
         ),
     )(
         prompt_hidden, prompt_keys, prompt_values, resp_hidden[0], resp_queries[0], resp_keys[0],
@@ -909,12 +890,11 @@
         name="widen",
         out_shape=(jax.ShapeDtypeStruct((RL, HQ * HD), BF16),)
         + tuple(jax.ShapeDtypeStruct(x, F32) for x in shapes),
-        in_specs=[hbm, hbm],
+        in_specs=[vmem, vmem],
         out_specs=(hbm,) * 5,
-        scratch_shapes=[pltpu.VMEM(gath_shape, BF16)]
-        + [pltpu.VMEM(x, F32) for x in shapes]
-        + [dma((8,)), dma((16,)), dma],
-        compiler_params=pltpu.CompilerParams(vmem_limit_bytes=60 * 2**20),
+        scratch_shapes=[pltpu.VMEM(x, F32) for x in shapes]
+        + [dma((16,)), dma],
+        compiler_params=pltpu.CompilerParams(vmem_limit_bytes=40 * 2**20),
     )(gath, attn)
     return (
         attn[None],

time: 88.4 us -> 82.5 us (0.933)
  Pallas kernels: 85.7 us -> 79.8 us
    pallas_call x1, Pallas kernels: 80.4 us -> 77.1 us  [per_device(): pl.pallas_call(functools.partial(step_kernel, dims), name='step', out_sha...]
    pallas_call x1, Pallas kernels: 5.31 us -> 2.75 us  [per_device(): pl.pallas_call(functools.partial(widen_kernel, dims), name='widen', out_s...]
where the time goes in v3:
time: 82.5 us; the launch traced here: 82.4 us
  Pallas kernels  79.8 us (97%)
  between operations  2.58 us (3%)
    pallas_call x1, Pallas kernels, per_device(): pl.pallas_call(functools.partial(step_kernel, dims), name='step', out_sha...  77.1 us
    pallas_call x1, Pallas kernels, per_device(): pl.pallas_call(functools.partial(widen_kernel, dims), name='widen', out_s...  2.75 us

profile of v3, /device:TPU:1, one launch (start us, length us, event | category | flops | bytes accessed | tf_op | source)
XLA Modules:
  0.0 82.4 jit_solution(3598288832836132204)
XLA Ops:
  2.6 77.1 %step.1 = (bf16[64,1024]{1,0:T(8,128)(2,1)S(1)}, bf16[2,2,2,4,4,2,3,16,128]{8,7,6,5,4,3,2,1,0:T(8,128)(2,1)S(1)}) custom-call(bf16[2,96,5120]{2,1,0:T(8,128)(2,1)} %ph_hbm.1, bf16[2,96,128]{2,1,0:T(8,128)(2,1)} %pk_hbm.1, bf16[2,96,128]{2,1,0:T(8,128)(2,1)} %pv_hbm.1, bf16[64,5120]{1,0:T(8,128)(2,1)} %bitcast.12, bf16[64,1024]{1,0:T(8,128)(2,1)} %bitcast.13, ...), custom_call_target="tpu_custom_call" | custom-call | tf_op jit(solution)/shard_map/step/pallas_call | solution.py:809
  79.6 2.7 %widen.1 = (bf16[64,1024]{1,0:T(8,128)(2,1)}, f32[8,16,5120]{2,1,0:T(8,128)}, f32[8,16,1024]{2,1,0:T(8,128)}, f32[8,16,5120]{2,1,0:T(8,128)}, f32[8,16,128]{2,1,0:T(8,128)}) custom-call(bf16[2,2,2,4,4,2,3,16,128]{8,7,6,5,4,3,2,1,0:T(8,128)(2,1)S(1)} %get-tuple-element.12.gath, bf16[64,1024]{1,0:T(8,128)(2,1)S(1)} %get-tuple-element.13.attn_in), custom_call_target="tpu_custom_call" | custom-call | tf_op jit(solution)/shard_map/widen/pallas_call | solution.py:888

commit v4 on v3

--- a/solution.py
+++ b/solution.py
@@ -556,6 +556,8 @@
     dov = dot_tn(e_own16, un[0]).astype(BF16)
     vb = dot_nt(v_up, dov).astype(BF16)
     vterm[...] = 2.0 * dot_nn(vb, rh[...])
+    for c in range(4):
+        s_scr[c] = dot_nt(un[0], v_scr[c, :, 0:HD])
     vp.finish()
     values(1)
 
@@ -580,7 +582,7 @@
         if c % 4 == 0:
             m_scr[...] = jnp.broadcast_to(delta * scale[half], (rows, HD))
         e16 = e_scr[c]
-        dp = dot_nt(un[half], v_scr[c, :, 0:HD])
+        dp = s_scr[c] if half == 0 else dot_nt(un[1], v_scr[c, :, 0:HD])
         db = m_scr[...]
         ds = jnp.concatenate(
             [

time: 82.5 us -> 82.6 us (level)
  no operation moved by 1% of the time
where the time goes in v4:
time: 82.6 us; the launch traced here: 82.5 us
  Pallas kernels  79.9 us (97%)
  between operations  2.58 us (3%)
    pallas_call x1, Pallas kernels, per_device(): pl.pallas_call(functools.partial(step_kernel, dims), name='step', out_sha...  77.1 us
    pallas_call x1, Pallas kernels, per_device(): pl.pallas_call(functools.partial(widen_kernel, dims), name='widen', out_s...  2.75 us

profile of v4, /device:TPU:1, one launch (start us, length us, event | category | flops | bytes accessed | tf_op | source)
XLA Modules:
  0.0 82.5 jit_solution(8184488147747575145)
XLA Ops:
  2.6 77.1 %step.1 = (bf16[64,1024]{1,0:T(8,128)(2,1)S(1)}, bf16[2,2,2,4,4,2,3,16,128]{8,7,6,5,4,3,2,1,0:T(8,128)(2,1)S(1)}) custom-call(bf16[2,96,5120]{2,1,0:T(8,128)(2,1)} %ph_hbm.1, bf16[2,96,128]{2,1,0:T(8,128)(2,1)} %pk_hbm.1, bf16[2,96,128]{2,1,0:T(8,128)(2,1)} %pv_hbm.1, bf16[64,5120]{1,0:T(8,128)(2,1)} %bitcast.12, bf16[64,1024]{1,0:T(8,128)(2,1)} %bitcast.13, ...), custom_call_target="tpu_custom_call" | custom-call | tf_op jit(solution)/shard_map/step/pallas_call | solution.py:811
  79.7 2.7 %widen.1 = (bf16[64,1024]{1,0:T(8,128)(2,1)}, f32[8,16,5120]{2,1,0:T(8,128)}, f32[8,16,1024]{2,1,0:T(8,128)}, f32[8,16,5120]{2,1,0:T(8,128)}, f32[8,16,128]{2,1,0:T(8,128)}) custom-call(bf16[2,2,2,4,4,2,3,16,128]{8,7,6,5,4,3,2,1,0:T(8,128)(2,1)S(1)} %get-tuple-element.12.gath, bf16[64,1024]{1,0:T(8,128)(2,1)S(1)} %get-tuple-element.13.attn_in), custom_call_target="tpu_custom_call" | custom-call | tf_op jit(solution)/shard_map/widen/pallas_call | solution.py:890
